TPU v7x, 256 devices: a whole 4x4x8 slice. The times are simulated.
256 devices in a mesh: slab: 64 (over z, y, core), grp: 4 (over x).
Axes of the slice: x: 4, y: 4, z: 8, core: 2. Of those that a mesh axis runs over, the one named last changes fastest.
Arguments:
- positions: float32 [256, 3, 8192], P(('slab', 'grp')), may hold values from 0 to 1
- masses: float32 [256, 8192], P(('slab', 'grp')), may hold values from 0.001 to 0.01
- smoothing: float32 [256, 8192], P(('slab', 'grp')), may hold values from 0.3 to 0.6
- block_lists: int32 [256, 64, 8], P(('slab', 'grp')), may hold values from 0 to 63, as said below
- block_counts: int32 [256, 64], P(('slab', 'grp')), may hold values from 0 to 128, as said below
- group_owner: int32 [4, 64], P('grp'), may hold values from 0 to 63, each once within a row
Outputs:
- density: float32 [256, 8192], P(('slab', 'grp'))
- potential: float32 [256, 8192], P(('slab', 'grp'))
- group_energy: float32 [4, 64], P('grp', 'slab')
Inputs may be any that keep to these rules, and one draw needn't show every extreme that they name: `block_lists`: columns 0 to 1 name blocks of the slab below, the next 4 columns blocks of the own slab, the first of them the block itself, and the last 2 columns blocks of the slab above; the entries of each of these three sets differ. Block c of a slab lists block b of the slab below in its first 2 columns exactly when block b lists block c in its last 2 columns. `block_counts`: within one subgroup, a slab's rows begin with the members of its groups, group after group in order of group number. In every subgroup one group has 128 members on every slab.
All inputs are finite; a program needn't handle non-finite values.
Results may differ from a plain program's by a relative error of at most 0.0003.
Values sent between devices are 32-bit elements; how exact they have to be, the bound alone decides.
No kernel may reach another device: no remote copies, remote signals or barrier semaphores. Data moves between devices by JAX's collectives and lax.ppermute only.
A program may use at most 64 MiB of HBM per device.

v0:
```python
import math

import jax
import jax.numpy as jnp
from jax import lax
from jax.sharding import PartitionSpec as P

TILE = 128
KX = 2
KO = 4


KERNEL_NORM = 21.0 / (16.0 * math.pi)


def extended_2(block, sides, width):
    for axis, dim in sides:
        count = lax.axis_size(axis)
        forward = [(i, i + 1) for i in range(count - 1)]
        forward.append((count - 1, 0))
        backward = [(target, source) for source, target in forward]
        low = lax.ppermute(
            lax.slice_in_dim(block, block.shape[dim] - width, None, axis=dim), axis, forward
        )
        high = lax.ppermute(lax.slice_in_dim(block, 0, width, axis=dim), axis, backward)
        block = jnp.concatenate([low, block, high], axis=dim)
    return block


def kernel_tile(target, source):
    delta_x = target[..., 0, :, None] - source[..., 0, None, :]
    delta_y = target[..., 1, :, None] - source[..., 1, None, :]
    delta_z = target[..., 2, :, None] - source[..., 2, None, :]
    pair_size = 0.5 * (target[..., 4, :, None] + source[..., 4, None, :])
    scaled = jnp.sqrt(delta_x * delta_x + delta_y * delta_y + delta_z * delta_z) / pair_size
    falloff = jnp.maximum(1.0 - 0.5 * scaled, 0.0)
    falloff_sq = falloff * falloff
    return (
        KERNEL_NORM
        / (pair_size * pair_size * pair_size)
        * falloff_sq
        * falloff_sq
        * (1.0 + 2.0 * scaled)
    )


def to_blocks(particles, tile_rows):
    return particles.reshape(5, -1, tile_rows).transpose(1, 0, 2)


def block_rows(targets, sources):
    weights = kernel_tile(targets[:, None], sources)
    return jnp.sum(weights * sources[:, :, 3, None, :], axis=(1, 3))


def potential_all(members):
    total_rows = members.shape[1]
    width = min(512, total_rows)
    softness = 0.25 * members[4] * members[4]

    def row_block(start):
        target = lax.dynamic_slice_in_dim(members, start, width, 1)
        target_soft = lax.dynamic_slice_in_dim(softness, start, width, 0)
        delta_x = target[0][:, None] - members[0][None, :]
        delta_y = target[1][:, None] - members[1][None, :]
        delta_z = target[2][:, None] - members[2][None, :]
        inverse = lax.rsqrt(
            delta_x * delta_x
            + delta_y * delta_y
            + delta_z * delta_z
            + 0.5 * (target_soft[:, None] + softness[None, :])
        )
        summed = jnp.sum(inverse * members[3][None, :], axis=1)
        return target[3] * lax.rsqrt(target_soft) - summed

    starts = jnp.arange(total_rows // width, dtype=jnp.int32) * width
    return lax.map(row_block, starts).reshape(total_rows)


def per_device(positions, masses, smoothing, block_lists, block_counts, group_owner):
    particles = jnp.concatenate([positions[0], masses, smoothing], axis=0)
    row_count = particles.shape[1]
    tile_rows = TILE
    block_total = row_count // tile_rows
    own_blocks = to_blocks(particles, tile_rows)
    slab_lists = block_lists[0]
    offset_x = jnp.array([1.0, 0.0, 0.0, 0.0, 0.0], jnp.float32)[:, None]
    loop_turns = 8
    per_turn = block_total // loop_turns
    turn_targets = own_blocks.reshape(loop_turns, per_turn, 5, tile_rows)
    extended = extended_2(particles[None], ((("slab", "grp"), 0),), 1)
    candidates = jnp.concatenate(
        [
            to_blocks(extended[0] - offset_x, tile_rows),
            own_blocks,
            to_blocks(extended[2] + offset_x, tile_rows),
        ],
        axis=0,
    )
    column_base = jnp.concatenate(
        [
            jnp.zeros((KX,), jnp.int32),
            jnp.full((KO,), block_total, jnp.int32),
            jnp.full((KX,), 2 * block_total, jnp.int32),
        ]
    )
    chosen = (slab_lists + column_base[None, :]).reshape(loop_turns, per_turn, -1)

    def pull_turn(pieces):
        targets, picks = pieces
        return block_rows(targets, candidates[picks])

    density = lax.map(pull_turn, (turn_targets, chosen)).reshape(row_count)
    counts = block_counts[0]
    owners = group_owner[0]
    groups_here = counts.shape[0]
    offsets = jnp.cumsum(counts) - counts
    labels = jnp.arange(groups_here, dtype=jnp.int32)
    owned_by = owners[:, None] == labels[None, :]
    slot_start = jnp.sum(jnp.where(owned_by, offsets[:, None], 0), axis=0)
    slot_count = jnp.sum(jnp.where(owned_by, counts[:, None], 0), axis=0)
    slot = jnp.arange(tile_rows, dtype=jnp.int32)
    row_index = jnp.minimum(slot_start[:, None] + slot[None, :], row_count - 1)
    live = slot[None, :] < slot_count[:, None]
    picked = jnp.take(particles, row_index.reshape(-1), axis=1).reshape(5, groups_here, tile_rows)
    masked = jnp.where(live, picked[3], 0.0)
    outgoing = jnp.concatenate([picked[:3], masked[None], picked[4:]], axis=0)
    members = lax.all_to_all(outgoing, "slab", split_axis=1, concat_axis=1, tiled=True).reshape(
        5, -1
    )
    values = potential_all(members)
    energy = 0.5 * jnp.sum(members[3] * values)
    sources = lax.axis_size("slab")
    returned = lax.all_to_all(
        values.reshape(sources, tile_rows), "slab", split_axis=0, concat_axis=0, tiled=True
    ).reshape(-1)
    ends = offsets + counts
    all_rows = jnp.arange(row_count, dtype=jnp.int32)
    member_of = jnp.sum((ends[None, :] <= all_rows[:, None]).astype(jnp.int32), axis=1)
    matched = member_of[:, None] == labels[None, :]
    row_owner = jnp.sum(jnp.where(matched, owners[None, :], 0), axis=1)
    row_start = jnp.sum(jnp.where(matched, offsets[None, :], 0), axis=1)
    flat_index = row_owner * tile_rows + jnp.clip(all_rows - row_start, 0, tile_rows - 1)
    potential = jnp.where(member_of < groups_here, returned[flat_index], 0.0)
    return (density[None], potential[None], energy.reshape(1, 1))


def solution(mesh):
    placed = (
        P(("slab", "grp"), None, None),
        P(("slab", "grp"), None),
        P(("slab", "grp"), None),
        P(("slab", "grp"), None, None),
        P(("slab", "grp"), None),
        P("grp", None),
    )
    return jax.shard_map(
        per_device,
        mesh=mesh,
        in_specs=placed,
        out_specs=(P(("slab", "grp"), None), P(("slab", "grp"), None), P("grp", "slab")),
        check_vma=False,
    )
```

profile of v0, /device:TPU:1, one launch (start us, length us, event | category | flops | bytes accessed | tf_op | source)
XLA Modules:
  0.0 366.9 jit_solution(14398832458013588105)
XLA Ops:
  0.7 1.0 copy.53
  1.6 0.9 pad_maximum_fusion.1
  2.6 4.0 %collective-permute-start.1 = (f32[1,5,8192]{2,0,1:T(1,128)S(1)}, f32[1,5,8192]{2,0,1:T(1,128)S(1)}, u32[]{:S(2)}, u32[]{:S(2)}) collective-permute-start(f32[1,5,8192]{2,0,1:T(1,128)S(1)} %broadcast_in_dim.95), channel_id=1, source_target_pairs={{1,0},{2,1},{3,2},{4,3},{5,4},{6,5},{7,6},{8,7},{9,8},{10,9},{11,1... | collective-permute-start | bytes 491528 | tf_op jit(solution)/shard_map/ppermute | solution.py:25
  6.6 2.6 copy.44
  9.9 29.9 %gather_fusion.1 = f32[8192,5]{1,0:T(8,128)} fusion(f32[5,8192]{0,1:T(8,128)} %copy.44, s32[8192]{0:T(1024)S(1)} %broadcast_clamp_fusion.1), kind=kCustom, calls=%fused_computation.1 | custom fusion | bytes 360448 | tf_op jit(solution)/shard_map/jit(_take)/gather | solution.py:125
  39.8 6.2 %select_bitcast_fusion = f32[5,8192]{0,1:T(8,128)S(1)} fusion(f32[8192,5]{1,0:T(8,128)} %gather_fusion.1, pred[8192]{0:T(1024)(128)(4,1)S(1)} %compare_and_fusion), kind=kLoop, calls=%fused_computation.22 | loop fusion | flops 40960 | bytes 335872 | tf_op jit(solution)/shard_map/jit(_take)/select_n | solution.py:125
  46.0 4.4 %slice_reduce_fusion.1 = (f32[8192]{0:T(1024)S(1)}, f32[8192]{0:T(1024)S(1)}) fusion(f32[5,8192]{0,1:T(8,128)S(1)} %select_bitcast_fusion), kind=kLoop, calls=%fused_computation.21 | loop fusion | bytes 131072 | tf_op jit(solution)/shard_map/slice | solution.py:126
  50.5 2.9 copy.45
  53.5 0.8 pad_maximum_fusion.2
  54.3 11.8 %all-to-all-start = ((f32[5,64,128]{2,0,1:T(8,128)}), f32[5,64,128]{2,0,1:T(8,128)S(1)}, u32[]{:S(2)}, u32[]{:S(2)}) async-start(f32[5,64,128]{2,0,1:T(8,128)} %pad_maximum_fusion.2), calls=%async_computation | async-start | bytes 524288 | tf_op jit(solution)/shard_map/all_to_all | solution.py:128
  67.9 52.5 %while.20 = (s32[]{:T(128)}, f32[8,8,128]{2,1,0:T(8,128)S(1)}, f32[8,8,5,128]{3,1,0,2:T(8,128)S(1)}, s32[8,8,8]{2,1,0:T(8,128)S(1)}, f32[192,5,128]{2,1,0:T(8,128)S(1)}, /*index=5*/s32[]{:T(128)}) while((s32[]{:T(128)}, f32[8,8,128]{2,1,0:T(8,128)S(1)}, f32[8,8,5,128]{3,1,0,2:T(8,128)S(1)}, s32[8,8,8]{2,1,0:T(8,128)S(1)}, ...), condition=%wide.region_2.3_spmd, body=%wide.region_0.2_spmd.sunk | while | flops 26214592 | bytes 927321 | solution.py:113
  68.0 0.6 gather_fusion
  68.8 5.6 %fusion.16 = f32[8,128]{1,0:T(8,128)S(1)} fusion(f32[8,8,128]{2,1,0:T(8,128)S(1)} %bitcast.139, f32[8,8,128]{2,1,0:T(8,128)S(1)} %bitcast.136, f32[8,128]{1,0:T(8,128)S(1)} %get-tuple-element.195, f32[8,8,128]{2,1,0:T(8,128)S(1)} %bitcast.137, f32[8,128]{1,0:T(8,128)S(1)} %get-tuple-element.197, f32[8,8,128]{2,1,0:T(8,128)S(1)} %bitcast.138, ...), kind=kLoop, calls=%fused_computation.11.clone.1 | loop fusion | flops 26213376 | bytes 184320 | tf_op jit(solution)/shard_map/while/body/eval_jaxpr/reduce_sum | solution.py:53
  74.6 0.6 gather_fusion
  75.4 5.6 %fusion.16 = f32[8,128]{1,0:T(8,128)S(1)} fusion(f32[8,8,128]{2,1,0:T(8,128)S(1)} %bitcast.139, f32[8,8,128]{2,1,0:T(8,128)S(1)} %bitcast.136, f32[8,128]{1,0:T(8,128)S(1)} %get-tuple-element.195, f32[8,8,128]{2,1,0:T(8,128)S(1)} %bitcast.137, f32[8,128]{1,0:T(8,128)S(1)} %get-tuple-element.197, f32[8,8,128]{2,1,0:T(8,128)S(1)} %bitcast.138, ...), kind=kLoop, calls=%fused_computation.11.clone.1 | loop fusion | flops 26213376 | bytes 184320 | tf_op jit(solution)/shard_map/while/body/eval_jaxpr/reduce_sum | solution.py:53
  81.2 0.6 gather_fusion
  82.0 5.6 %fusion.16 = f32[8,128]{1,0:T(8,128)S(1)} fusion(f32[8,8,128]{2,1,0:T(8,128)S(1)} %bitcast.139, f32[8,8,128]{2,1,0:T(8,128)S(1)} %bitcast.136, f32[8,128]{1,0:T(8,128)S(1)} %get-tuple-element.195, f32[8,8,128]{2,1,0:T(8,128)S(1)} %bitcast.137, f32[8,128]{1,0:T(8,128)S(1)} %get-tuple-element.197, f32[8,8,128]{2,1,0:T(8,128)S(1)} %bitcast.138, ...), kind=kLoop, calls=%fused_computation.11.clone.1 | loop fusion | flops 26213376 | bytes 184320 | tf_op jit(solution)/shard_map/while/body/eval_jaxpr/reduce_sum | solution.py:53
  87.7 0.6 gather_fusion
  88.5 5.6 %fusion.16 = f32[8,128]{1,0:T(8,128)S(1)} fusion(f32[8,8,128]{2,1,0:T(8,128)S(1)} %bitcast.139, f32[8,8,128]{2,1,0:T(8,128)S(1)} %bitcast.136, f32[8,128]{1,0:T(8,128)S(1)} %get-tuple-element.195, f32[8,8,128]{2,1,0:T(8,128)S(1)} %bitcast.137, f32[8,128]{1,0:T(8,128)S(1)} %get-tuple-element.197, f32[8,8,128]{2,1,0:T(8,128)S(1)} %bitcast.138, ...), kind=kLoop, calls=%fused_computation.11.clone.1 | loop fusion | flops 26213376 | bytes 184320 | tf_op jit(solution)/shard_map/while/body/eval_jaxpr/reduce_sum | solution.py:53
  94.3 0.6 gather_fusion
  95.1 5.6 %fusion.16 = f32[8,128]{1,0:T(8,128)S(1)} fusion(f32[8,8,128]{2,1,0:T(8,128)S(1)} %bitcast.139, f32[8,8,128]{2,1,0:T(8,128)S(1)} %bitcast.136, f32[8,128]{1,0:T(8,128)S(1)} %get-tuple-element.195, f32[8,8,128]{2,1,0:T(8,128)S(1)} %bitcast.137, f32[8,128]{1,0:T(8,128)S(1)} %get-tuple-element.197, f32[8,8,128]{2,1,0:T(8,128)S(1)} %bitcast.138, ...), kind=kLoop, calls=%fused_computation.11.clone.1 | loop fusion | flops 26213376 | bytes 184320 | tf_op jit(solution)/shard_map/while/body/eval_jaxpr/reduce_sum | solution.py:53
  101.6 5.6 %fusion.16 = f32[8,128]{1,0:T(8,128)S(1)} fusion(f32[8,8,128]{2,1,0:T(8,128)S(1)} %bitcast.139, f32[8,8,128]{2,1,0:T(8,128)S(1)} %bitcast.136, f32[8,128]{1,0:T(8,128)S(1)} %get-tuple-element.195, f32[8,8,128]{2,1,0:T(8,128)S(1)} %bitcast.137, f32[8,128]{1,0:T(8,128)S(1)} %get-tuple-element.197, f32[8,8,128]{2,1,0:T(8,128)S(1)} %bitcast.138, ...), kind=kLoop, calls=%fused_computation.11.clone.1 | loop fusion | flops 26213376 | bytes 184320 | tf_op jit(solution)/shard_map/while/body/eval_jaxpr/reduce_sum | solution.py:53
  107.4 0.6 gather_fusion
  108.2 5.6 %fusion.16 = f32[8,128]{1,0:T(8,128)S(1)} fusion(f32[8,8,128]{2,1,0:T(8,128)S(1)} %bitcast.139, f32[8,8,128]{2,1,0:T(8,128)S(1)} %bitcast.136, f32[8,128]{1,0:T(8,128)S(1)} %get-tuple-element.195, f32[8,8,128]{2,1,0:T(8,128)S(1)} %bitcast.137, f32[8,128]{1,0:T(8,128)S(1)} %get-tuple-element.197, f32[8,8,128]{2,1,0:T(8,128)S(1)} %bitcast.138, ...), kind=kLoop, calls=%fused_computation.11.clone.1 | loop fusion | flops 26213376 | bytes 184320 | tf_op jit(solution)/shard_map/while/body/eval_jaxpr/reduce_sum | solution.py:53
  113.9 0.6 gather_fusion
  114.7 5.6 %fusion.16 = f32[8,128]{1,0:T(8,128)S(1)} fusion(f32[8,8,128]{2,1,0:T(8,128)S(1)} %bitcast.139, f32[8,8,128]{2,1,0:T(8,128)S(1)} %bitcast.136, f32[8,128]{1,0:T(8,128)S(1)} %get-tuple-element.195, f32[8,8,128]{2,1,0:T(8,128)S(1)} %bitcast.137, f32[8,128]{1,0:T(8,128)S(1)} %get-tuple-element.197, f32[8,8,128]{2,1,0:T(8,128)S(1)} %bitcast.138, ...), kind=kLoop, calls=%fused_computation.11.clone.1 | loop fusion | flops 26213376 | bytes 184320 | tf_op jit(solution)/shard_map/while/body/eval_jaxpr/reduce_sum | solution.py:53
  121.0 178.2 %while.21 = (s32[]{:T(128)}, f32[16,512]{1,0:T(8,128)S(1)}, s32[16]{0:T(128)S(1)}, f32[5,8192]{1,0:T(8,128)S(1)}, f32[8192]{0:T(1024)S(1)}, /*index=5*/s32[]{:T(...) while((s32[]{:T(128)}, f32[16,512]{1,0:T(8,128)S(1)}, s32[16]{0:T(128)S(1)}, f32[5,8192]{1,0:T(8,128)S(1)}, ...), condition=%wide.region_9.10_spmd, body=%wide.region_7.9_spmd.sunk | while | flops 54526472 | bytes 469219 | solution.py:77
  123.8 8.2 %multiply_reduce_fusion.2 = f32[512]{0:T(512)S(1)} fusion(f32[8192]{0:T(1024)S(1)} %bitcast.141, f32[8192]{0:T(1024)S(1)} %get-tuple-element.259, f32[512]{0:T(512)S(1)} %dynamic_slice.30, f32[8192]{0:T(1024)S(1)} %bitcast.142, f32[512]{0:T(512)S(1)} %bitcast.162, f32[8192]{0:T(1024)S(1)} %bitcast.143, f32[512]{0:T(512)S(1)} %bitcast.160, ...), kind=kLoop, calls=%fused_computation.3.clone.1 | loop fusion | flops 54525440 | bytes 174080 | tf_op jit(solution)/shard_map/while/body/eval_jaxpr/reduce_sum | solution.py:73
  134.9 8.2 %multiply_reduce_fusion.2 = f32[512]{0:T(512)S(1)} fusion(f32[8192]{0:T(1024)S(1)} %bitcast.141, f32[8192]{0:T(1024)S(1)} %get-tuple-element.259, f32[512]{0:T(512)S(1)} %dynamic_slice.30, f32[8192]{0:T(1024)S(1)} %bitcast.142, f32[512]{0:T(512)S(1)} %bitcast.162, f32[8192]{0:T(1024)S(1)} %bitcast.143, f32[512]{0:T(512)S(1)} %bitcast.160, ...), kind=kLoop, calls=%fused_computation.3.clone.1 | loop fusion | flops 54525440 | bytes 174080 | tf_op jit(solution)/shard_map/while/body/eval_jaxpr/reduce_sum | solution.py:73
  146.1 8.2 %multiply_reduce_fusion.2 = f32[512]{0:T(512)S(1)} fusion(f32[8192]{0:T(1024)S(1)} %bitcast.141, f32[8192]{0:T(1024)S(1)} %get-tuple-element.259, f32[512]{0:T(512)S(1)} %dynamic_slice.30, f32[8192]{0:T(1024)S(1)} %bitcast.142, f32[512]{0:T(512)S(1)} %bitcast.162, f32[8192]{0:T(1024)S(1)} %bitcast.143, f32[512]{0:T(512)S(1)} %bitcast.160, ...), kind=kLoop, calls=%fused_computation.3.clone.1 | loop fusion | flops 54525440 | bytes 174080 | tf_op jit(solution)/shard_map/while/body/eval_jaxpr/reduce_sum | solution.py:73
  157.2 8.2 %multiply_reduce_fusion.2 = f32[512]{0:T(512)S(1)} fusion(f32[8192]{0:T(1024)S(1)} %bitcast.141, f32[8192]{0:T(1024)S(1)} %get-tuple-element.259, f32[512]{0:T(512)S(1)} %dynamic_slice.30, f32[8192]{0:T(1024)S(1)} %bitcast.142, f32[512]{0:T(512)S(1)} %bitcast.162, f32[8192]{0:T(1024)S(1)} %bitcast.143, f32[512]{0:T(512)S(1)} %bitcast.160, ...), kind=kLoop, calls=%fused_computation.3.clone.1 | loop fusion | flops 54525440 | bytes 174080 | tf_op jit(solution)/shard_map/while/body/eval_jaxpr/reduce_sum | solution.py:73
  168.4 8.2 %multiply_reduce_fusion.2 = f32[512]{0:T(512)S(1)} fusion(f32[8192]{0:T(1024)S(1)} %bitcast.141, f32[8192]{0:T(1024)S(1)} %get-tuple-element.259, f32[512]{0:T(512)S(1)} %dynamic_slice.30, f32[8192]{0:T(1024)S(1)} %bitcast.142, f32[512]{0:T(512)S(1)} %bitcast.162, f32[8192]{0:T(1024)S(1)} %bitcast.143, f32[512]{0:T(512)S(1)} %bitcast.160, ...), kind=kLoop, calls=%fused_computation.3.clone.1 | loop fusion | flops 54525440 | bytes 174080 | tf_op jit(solution)/shard_map/while/body/eval_jaxpr/reduce_sum | solution.py:73
  179.5 8.2 %multiply_reduce_fusion.2 = f32[512]{0:T(512)S(1)} fusion(f32[8192]{0:T(1024)S(1)} %bitcast.141, f32[8192]{0:T(1024)S(1)} %get-tuple-element.259, f32[512]{0:T(512)S(1)} %dynamic_slice.30, f32[8192]{0:T(1024)S(1)} %bitcast.142, f32[512]{0:T(512)S(1)} %bitcast.162, f32[8192]{0:T(1024)S(1)} %bitcast.143, f32[512]{0:T(512)S(1)} %bitcast.160, ...), kind=kLoop, calls=%fused_computation.3.clone.1 | loop fusion | flops 54525440 | bytes 174080 | tf_op jit(solution)/shard_map/while/body/eval_jaxpr/reduce_sum | solution.py:73
  190.6 8.2 %multiply_reduce_fusion.2 = f32[512]{0:T(512)S(1)} fusion(f32[8192]{0:T(1024)S(1)} %bitcast.141, f32[8192]{0:T(1024)S(1)} %get-tuple-element.259, f32[512]{0:T(512)S(1)} %dynamic_slice.30, f32[8192]{0:T(1024)S(1)} %bitcast.142, f32[512]{0:T(512)S(1)} %bitcast.162, f32[8192]{0:T(1024)S(1)} %bitcast.143, f32[512]{0:T(512)S(1)} %bitcast.160, ...), kind=kLoop, calls=%fused_computation.3.clone.1 | loop fusion | flops 54525440 | bytes 174080 | tf_op jit(solution)/shard_map/while/body/eval_jaxpr/reduce_sum | solution.py:73
  201.8 8.2 %multiply_reduce_fusion.2 = f32[512]{0:T(512)S(1)} fusion(f32[8192]{0:T(1024)S(1)} %bitcast.141, f32[8192]{0:T(1024)S(1)} %get-tuple-element.259, f32[512]{0:T(512)S(1)} %dynamic_slice.30, f32[8192]{0:T(1024)S(1)} %bitcast.142, f32[512]{0:T(512)S(1)} %bitcast.162, f32[8192]{0:T(1024)S(1)} %bitcast.143, f32[512]{0:T(512)S(1)} %bitcast.160, ...), kind=kLoop, calls=%fused_computation.3.clone.1 | loop fusion | flops 54525440 | bytes 174080 | tf_op jit(solution)/shard_map/while/body/eval_jaxpr/reduce_sum | solution.py:73
  212.9 8.2 %multiply_reduce_fusion.2 = f32[512]{0:T(512)S(1)} fusion(f32[8192]{0:T(1024)S(1)} %bitcast.141, f32[8192]{0:T(1024)S(1)} %get-tuple-element.259, f32[512]{0:T(512)S(1)} %dynamic_slice.30, f32[8192]{0:T(1024)S(1)} %bitcast.142, f32[512]{0:T(512)S(1)} %bitcast.162, f32[8192]{0:T(1024)S(1)} %bitcast.143, f32[512]{0:T(512)S(1)} %bitcast.160, ...), kind=kLoop, calls=%fused_computation.3.clone.1 | loop fusion | flops 54525440 | bytes 174080 | tf_op jit(solution)/shard_map/while/body/eval_jaxpr/reduce_sum | solution.py:73
  224.1 8.2 %multiply_reduce_fusion.2 = f32[512]{0:T(512)S(1)} fusion(f32[8192]{0:T(1024)S(1)} %bitcast.141, f32[8192]{0:T(1024)S(1)} %get-tuple-element.259, f32[512]{0:T(512)S(1)} %dynamic_slice.30, f32[8192]{0:T(1024)S(1)} %bitcast.142, f32[512]{0:T(512)S(1)} %bitcast.162, f32[8192]{0:T(1024)S(1)} %bitcast.143, f32[512]{0:T(512)S(1)} %bitcast.160, ...), kind=kLoop, calls=%fused_computation.3.clone.1 | loop fusion | flops 54525440 | bytes 174080 | tf_op jit(solution)/shard_map/while/body/eval_jaxpr/reduce_sum | solution.py:73
  235.2 8.2 %multiply_reduce_fusion.2 = f32[512]{0:T(512)S(1)} fusion(f32[8192]{0:T(1024)S(1)} %bitcast.141, f32[8192]{0:T(1024)S(1)} %get-tuple-element.259, f32[512]{0:T(512)S(1)} %dynamic_slice.30, f32[8192]{0:T(1024)S(1)} %bitcast.142, f32[512]{0:T(512)S(1)} %bitcast.162, f32[8192]{0:T(1024)S(1)} %bitcast.143, f32[512]{0:T(512)S(1)} %bitcast.160, ...), kind=kLoop, calls=%fused_computation.3.clone.1 | loop fusion | flops 54525440 | bytes 174080 | tf_op jit(solution)/shard_map/while/body/eval_jaxpr/reduce_sum | solution.py:73
  246.4 8.2 %multiply_reduce_fusion.2 = f32[512]{0:T(512)S(1)} fusion(f32[8192]{0:T(1024)S(1)} %bitcast.141, f32[8192]{0:T(1024)S(1)} %get-tuple-element.259, f32[512]{0:T(512)S(1)} %dynamic_slice.30, f32[8192]{0:T(1024)S(1)} %bitcast.142, f32[512]{0:T(512)S(1)} %bitcast.162, f32[8192]{0:T(1024)S(1)} %bitcast.143, f32[512]{0:T(512)S(1)} %bitcast.160, ...), kind=kLoop, calls=%fused_computation.3.clone.1 | loop fusion | flops 54525440 | bytes 174080 | tf_op jit(solution)/shard_map/while/body/eval_jaxpr/reduce_sum | solution.py:73
  257.5 8.2 %multiply_reduce_fusion.2 = f32[512]{0:T(512)S(1)} fusion(f32[8192]{0:T(1024)S(1)} %bitcast.141, f32[8192]{0:T(1024)S(1)} %get-tuple-element.259, f32[512]{0:T(512)S(1)} %dynamic_slice.30, f32[8192]{0:T(1024)S(1)} %bitcast.142, f32[512]{0:T(512)S(1)} %bitcast.162, f32[8192]{0:T(1024)S(1)} %bitcast.143, f32[512]{0:T(512)S(1)} %bitcast.160, ...), kind=kLoop, calls=%fused_computation.3.clone.1 | loop fusion | flops 54525440 | bytes 174080 | tf_op jit(solution)/shard_map/while/body/eval_jaxpr/reduce_sum | solution.py:73
  268.6 8.2 %multiply_reduce_fusion.2 = f32[512]{0:T(512)S(1)} fusion(f32[8192]{0:T(1024)S(1)} %bitcast.141, f32[8192]{0:T(1024)S(1)} %get-tuple-element.259, f32[512]{0:T(512)S(1)} %dynamic_slice.30, f32[8192]{0:T(1024)S(1)} %bitcast.142, f32[512]{0:T(512)S(1)} %bitcast.162, f32[8192]{0:T(1024)S(1)} %bitcast.143, f32[512]{0:T(512)S(1)} %bitcast.160, ...), kind=kLoop, calls=%fused_computation.3.clone.1 | loop fusion | flops 54525440 | bytes 174080 | tf_op jit(solution)/shard_map/while/body/eval_jaxpr/reduce_sum | solution.py:73
  279.8 8.2 %multiply_reduce_fusion.2 = f32[512]{0:T(512)S(1)} fusion(f32[8192]{0:T(1024)S(1)} %bitcast.141, f32[8192]{0:T(1024)S(1)} %get-tuple-element.259, f32[512]{0:T(512)S(1)} %dynamic_slice.30, f32[8192]{0:T(1024)S(1)} %bitcast.142, f32[512]{0:T(512)S(1)} %bitcast.162, f32[8192]{0:T(1024)S(1)} %bitcast.143, f32[512]{0:T(512)S(1)} %bitcast.160, ...), kind=kLoop, calls=%fused_computation.3.clone.1 | loop fusion | flops 54525440 | bytes 174080 | tf_op jit(solution)/shard_map/while/body/eval_jaxpr/reduce_sum | solution.py:73
  290.9 8.2 %multiply_reduce_fusion.2 = f32[512]{0:T(512)S(1)} fusion(f32[8192]{0:T(1024)S(1)} %bitcast.141, f32[8192]{0:T(1024)S(1)} %get-tuple-element.259, f32[512]{0:T(512)S(1)} %dynamic_slice.30, f32[8192]{0:T(1024)S(1)} %bitcast.142, f32[512]{0:T(512)S(1)} %bitcast.162, f32[8192]{0:T(1024)S(1)} %bitcast.143, f32[512]{0:T(512)S(1)} %bitcast.160, ...), kind=kLoop, calls=%fused_computation.3.clone.1 | loop fusion | flops 54525440 | bytes 174080 | tf_op jit(solution)/shard_map/while/body/eval_jaxpr/reduce_sum | solution.py:73
  299.3 0.7 all_to_all.10
  300.0 10.3 %all-to-all-start.1 = ((f32[64,1,128]{2,1,0:T(1,128)}), f32[64,1,128]{2,1,0:T(1,128)S(1)}, u32[]{:S(2)}, u32[]{:S(2)}) async-start(f32[64,1,128]{2,1,0:T(1,128)} %all_to_all.10), calls=%async_computation.1 | async-start | bytes 65536 | tf_op jit(solution)/shard_map/all_to_all | solution.py:134
  310.3 0.7 fusion.6
  311.6 8.0 %all-to-all-done.1 = f32[64,1,128]{2,1,0:T(1,128)S(1)} async-done(((f32[64,1,128]{2,1,0:T(1,128)}), f32[64,1,128]{2,1,0:T(1,128)S(1)}, u32[]{:S(2)}, u32[]{:S(2)}) %all-to-all-start.1) | async-done | bytes 32800 | tf_op jit(solution)/shard_map/all_to_all | solution.py:134
  319.6 45.5 %gather_fusion.2 = f32[8192]{0:T(1024)S(1)} fusion(f32[8192]{0:T(1024)S(1)} %bitcast.130, s32[8192]{0:T(1024)S(1)} %broadcast_clamp_fusion), kind=kCustom, calls=%fused_computation.2 | custom fusion | bytes 98304 | tf_op jit(solution)/shard_map/gather | solution.py:144
  (210 shorter events, 21.8 us)
Async XLA Ops:
  0.6 8.6 %copy-start.5 = (s32[1,64]{1,0:T(1,128)S(1)}, s32[1,64]{1,0:T(1,128)}, u32[]{:S(2)}) copy-start(s32[1,64]{1,0:T(1,128)} %param.15) | copy-start | bytes 772
  0.6 8.9 %copy-start.6 = (s32[1,64]{1,0:T(1,128)S(1)}, s32[1,64]{1,0:T(1,128)}, u32[]{:S(2)}) copy-start(s32[1,64]{1,0:T(1,128)} %param.16) | copy-start | bytes 772
  2.6 64.7 %collective-permute-start.1 = (f32[1,5,8192]{2,0,1:T(1,128)S(1)}, f32[1,5,8192]{2,0,1:T(1,128)S(1)}, u32[]{:S(2)}, u32[]{:S(2)}) collective-permute-start(f32[1,5,8192]{2,0,1:T(1,128)S(1)} %broadcast_in_dim.95), channel_id=1, source_target_pairs={{1,0},{2,1},{3,2},{4,3},{5,4},{6,5},{7,6},{8,7},{9,8},{10,9},{11,1... | collective-permute-start | bytes 491528 | tf_op jit(solution)/shard_map/ppermute | solution.py:25
  6.6 60.9 %collective-permute-start = (f32[1,5,8192]{2,0,1:T(1,128)S(1)}, f32[1,5,8192]{2,0,1:T(1,128)S(1)}, u32[]{:S(2)}, u32[]{:S(2)}) collective-permute-start(f32[1,5,8192]{2,0,1:T(1,128)S(1)} %broadcast_in_dim.95), channel_id=1, source_target_pairs={{0,1},{1,2},{2,3},{3,4},{4,5},{5,6},{6,7},{7,8},{8,9},{9,10},{10,1... | collective-permute-start | bytes 491528 | tf_op jit(solution)/shard_map/ppermute | solution.py:22
  46.0 4.4 %copy-start = (f32[5,8192]{0,1:T(8,128)}, f32[5,8192]{0,1:T(8,128)S(1)}, u32[]{:S(2)}) copy-start(f32[5,8192]{0,1:T(8,128)S(1)} %select_bitcast_fusion) | copy-start | bytes 491524
  50.4 16.0 %copy-start.4 = (s32[1,64,8]{1,2,0:T(8,128)S(1)}, s32[1,64,8]{1,2,0:T(8,128)}, u32[]{:S(2)}) copy-start(s32[1,64,8]{1,2,0:T(8,128)} %param.14) | copy-start | bytes 6148
  50.4 16.8 %copy-start.9 = (s32[8]{0:T(128)S(1)}, s32[8]{0:T(128)}, u32[]{:S(2)}) copy-start(s32[8]{0:T(128)} %constant.45.clone.1) | copy-start | bytes 100
  50.5 16.8 %copy-start.1 = (f32[1,3,8192]{2,0,1:T(1,128)S(1)}, f32[1,3,8192]{2,0,1:T(1,128)}, u32[]{:S(2)}) copy-start(f32[1,3,8192]{2,0,1:T(1,128)} %param.11) | copy-start | bytes 294916
  50.5 16.8 %copy-start.2 = (f32[1,8192]{1,0:T(1,128)S(1)}, f32[1,8192]{1,0:T(1,128)}, u32[]{:S(2)}) copy-start(f32[1,8192]{1,0:T(1,128)} %param.13) | copy-start | bytes 98308
  50.5 16.8 %copy-start.3 = (f32[1,8192]{1,0:T(1,128)S(1)}, f32[1,8192]{1,0:T(1,128)}, u32[]{:S(2)}) copy-start(f32[1,8192]{1,0:T(1,128)} %param.12) | copy-start | bytes 98308
  50.5 16.9 %copy-start.8 = (f32[5]{0:T(128)S(1)}, f32[5]{0:T(128)}, u32[]{:S(2)}) copy-start(f32[5]{0:T(128)} %constant.67.clone) | copy-start | bytes 64
  50.5 17.0 %copy-start.7 = (f32[5]{0:T(128)S(1)}, f32[5]{0:T(128)}, u32[]{:S(2)}) copy-start(f32[5]{0:T(128)} %constant.90) | copy-start | bytes 64
  54.3 66.1 %all-to-all-start = ((f32[5,64,128]{2,0,1:T(8,128)}), f32[5,64,128]{2,0,1:T(8,128)S(1)}, u32[]{:S(2)}, u32[]{:S(2)}) async-start(f32[5,64,128]{2,0,1:T(8,128)} %pad_maximum_fusion.2), calls=%async_computation | async-start | bytes 524288 | tf_op jit(solution)/shard_map/all_to_all | solution.py:128
  120.4 0.6 copy-start.10
  300.0 19.6 %all-to-all-start.1 = ((f32[64,1,128]{2,1,0:T(1,128)}), f32[64,1,128]{2,1,0:T(1,128)S(1)}, u32[]{:S(2)}, u32[]{:S(2)}) async-start(f32[64,1,128]{2,1,0:T(1,128)} %all_to_all.10), calls=%async_computation.1 | async-start | bytes 65536 | tf_op jit(solution)/shard_map/all_to_all | solution.py:134
where the time goes:
time: 370 us; the launch traced here: 367 us
  other arithmetic  189 us (51%)
  local copies, waits for them, and re-layouts  109 us (29%)
  loops' own time  32.2 us (9%)
  starting transfers between devices  26 us (7%)
  waiting for transfers between devices  7.99 us (2%)
    reduce_sum x16, other arithmetic, row_block(): summed = jnp.sum(inverse * members[3][None, :], axis=1)  131 us
    gather x1, local copies, waits for them, and re-layouts, per_device(): potential = jnp.where(member_of < groups_here, returned[flat_index], 0.0)  45.5 us
    reduce_sum x8, other arithmetic, block_rows(): return jnp.sum(weights * sources[:, :, 3, None, :], axis=(1, 3))  45 us
    another operation x1, loops' own time, potential_all(): return lax.map(row_block, starts).reshape(total_rows)  31.6 us
    gather x1, local copies, waits for them, and re-layouts, per_device(): jnp.take(particles, row_index.reshape(-1), axis=1)  29.9 us
    all_to_all x1, starting transfers between devices, per_device(): lax.all_to_all(outgoing, 'slab', split_axis=1, concat_axis=1, tiled=True)  11.8 us
    all_to_all x1, starting transfers between devices, per_device(): lax.all_to_all(values.reshape(sources, tile_rows), 'slab', split_axis=0,...  10.3 us
    dynamic_slice x16, local copies, waits for them, and re-layouts, potential_all(): return lax.map(row_block, starts).reshape(total_rows)  9.42 us
  transfers between devices with their start and end apart: 4, of which 1 were waited for; matrix products, arithmetic and copies ran while one was open for 28% of the time, Pallas kernels for 0%

commit v1 on v0

v1 whole, which is shorter than its diff:
```python
import functools
import math

import jax
import jax.numpy as jnp
from jax import lax
from jax.experimental import pallas as pl
from jax.experimental.pallas import tpu as pltpu
from jax.sharding import PartitionSpec as P

TILE = 128
PB = 64
KX = 2
KO = 4
COLS = 2 * KX + KO
GROUPS = 64
STEP = 512
PER_STEP = STEP // TILE
STEPS = PB // PER_STEP
KERNEL_NORM = 21.0 / (16.0 * math.pi)
VMEM = pl.BlockSpec(memory_space=pltpu.VMEM)
SMEM = pl.BlockSpec(memory_space=pltpu.SMEM)


def params():
    return pltpu.CompilerParams(vmem_limit_bytes=48 * 1024 * 1024)


def lanes(shape):
    return lax.broadcasted_iota(jnp.int32, shape, len(shape) - 1)


def rows(shape):
    return lax.broadcasted_iota(jnp.int32, shape, len(shape) - 2)


def factors(coords, extra):
    row = rows(coords.shape)
    high = coords.astype(jnp.bfloat16).astype(jnp.float32)
    low = coords - high
    norm = jnp.sum(coords * coords, axis=0, keepdims=True) + extra
    norm = jnp.broadcast_to(norm, coords.shape)
    n0 = norm.astype(jnp.bfloat16).astype(jnp.float32)
    rest = norm - n0
    n1 = rest.astype(jnp.bfloat16).astype(jnp.float32)
    n2 = rest - n1
    one = jnp.where(row < 6, 1.0, 0.0)
    lead = jnp.where(row == 0, n0, jnp.where(row == 1, n1, jnp.where(row == 2, n2, one)))
    tail = jnp.where(row == 3, n0, jnp.where(row == 4, n1, jnp.where(row == 5, n2, one)))
    target = jnp.concatenate([high, high, low, lead], axis=0)
    source = jnp.concatenate([-2.0 * high, -2.0 * low, -2.0 * high, tail], axis=0)
    return target, source


def pack_kernel(counts, owners, pos, mass, smooth, blocks, message):
    for c in range(PB):
        cut = slice(c * TILE, (c + 1) * TILE)
        blocks[c, 0:3, :] = pos[0, :, cut]
        blocks[c, 3:4, :] = mass[:, cut]
        blocks[c, 4:5, :] = smooth[:, cut]
        blocks[c, 5:8, :] = jnp.zeros((3, TILE), jnp.float32)
    lane = lanes((8, TILE))
    row = rows((8, TILE))

    def window(start):
        q = jnp.minimum(start // TILE, PB - 1)
        r = start % TILE
        both = jnp.where(lane >= r, blocks[q], blocks[jnp.minimum(q + 1, PB - 1)])
        return pltpu.roll(both, (TILE - r) % TILE, 1)

    def group(k, carry):
        start, hot, hot_start = carry
        count = counts[0, k]
        value = window(start)
        value = jnp.where((row == 3) & (lane >= count), 0.0, value)
        value = jnp.where(row == 5, count.astype(jnp.float32), value)
        message[owners[0, k], 0:8, :] = value
        first = (count == TILE) & (hot < 0)
        return (
            start + count,
            jnp.where(first, k, hot),
            jnp.where(first, start, hot_start),
        )

    _, hot, hot_start = lax.fori_loop(
        0, GROUPS, group, (jnp.int32(0), jnp.int32(-1), jnp.int32(0)), unroll=8
    )
    value = jnp.where(row == 5, hot.astype(jnp.float32), window(hot_start))
    for d in range(GROUPS):
        message[d, 8:16, :] = value


def density_kernel(lists, own, below, above, out, source, target, props, d_even, d_odd, wide_even, wide_odd):
    row = rows((8, TILE))

    def prepare(ref, base, shift, with_target):
        def step(c, _):
            block = ref[c]
            coords = jnp.where(row < 3, block - 0.5, 0.0)
            if shift:
                coords = jnp.where(row == 0, coords + shift, coords)
            f, g = factors(coords, 0.0)
            source[base + c] = g.astype(jnp.bfloat16)
            props[base + c] = block
            if with_target:
                target[c] = f.T.astype(jnp.bfloat16)
            return 0

        lax.fori_loop(0, PB, step, 0, unroll=4)

    prepare(below, 0, -1.0, False)
    prepare(own, PB, 0.0, True)
    prepare(above, 2 * PB, 1.0, False)

    def pick(b, s):
        base = 0 if s < KX else (PB if s < KX + KO else 2 * PB)
        return lists[0, b, s] + base

    def distances(b, d_ref, wide):
        b = jnp.minimum(b, PB - 1)
        for s in range(0, COLS, 2):
            pair = jnp.concatenate([source[pick(b, s)], source[pick(b, s + 1)]], axis=1)
            d_ref[:, s * TILE : (s + 2) * TILE] = jnp.dot(
                target[b], pair, preferred_element_type=jnp.float32
            )
        wide[...] = jnp.broadcast_to(props[PB + b, 4:5, :], (TILE, TILE)).T

    def weigh(b, d_ref, wide):
        total = []
        hs = [props[pick(b, s), 4:5, :] for s in range(COLS)]
        ms = [props[pick(b, s), 3:4, :] * (8.0 * KERNEL_NORM) for s in range(COLS)]
        for r in range(0, TILE, 16):
            part = None
            mine = wide[r : r + 16, :]
            for s in range(COLS):
                d2 = jnp.maximum(d_ref[r : r + 16, s * TILE : (s + 1) * TILE], 1e-20)
                inverse = pl.reciprocal(mine + hs[s], approx=True)
                t = d2 * lax.rsqrt(d2) * inverse
                fall = jnp.maximum(1.0 - t, 0.0)
                fall = fall * fall
                fall = fall * fall
                value = (fall * (1.0 + 4.0 * t)) * (inverse * inverse * (inverse * ms[s]))
                part = value if part is None else part + value
            total.append(part)
        whole = jnp.concatenate(total, axis=0)
        out[pl.ds(b, 1), :] = jnp.sum(whole.T, axis=0, keepdims=True)

    distances(0, d_even, wide_even)

    def turn(i, _):
        b = 2 * i
        distances(b + 1, d_odd, wide_odd)
        weigh(b, d_even, wide_even)
        distances(b + 2, d_even, wide_even)
        weigh(b + 1, d_odd, wide_odd)
        return 0

    lax.fori_loop(0, PB // 2, turn, 0)


def potential_kernel(
    place, owners, got, back, hot_phi, energy, offs, dense, phis, source, target, mass, sums, d_even, d_odd
):
    me = place[0]
    lane = lanes((8, TILE))
    row = rows((8, TILE))
    labels = got[:, 13, :]
    least = jnp.min(labels)
    agreed = least == jnp.max(labels)
    hot = jnp.maximum(least.astype(jnp.int32), 0)
    mine = agreed & (owners[0, hot] == me)

    at = jnp.int32(0)
    held = jnp.zeros((8, TILE), jnp.float32)
    for s in range(PB):
        q, r = at // TILE, at % TILE
        offs[s] = at
        rolled = pltpu.roll(got[s, 0:8, :], r, 1)
        merged = jnp.where(lane < r, held, rolled)
        dense[q] = merged
        dense[q + 1] = rolled
        at = at + got[s, 5:6, 0:1][0, 0].astype(jnp.int32)
        held = jnp.where(at // TILE == q, merged, rolled)
    total = at
    total = jnp.where(mine, 0, total)
    n_targets = (total + TILE - 1) // TILE
    n_steps = (total + STEP - 1) // STEP

    def prepare(block, c_step, c_lane, c_target, valid):
        block = jnp.where(valid, block, jnp.where(row == 4, 1.0, 0.0))
        coords = jnp.where(row < 3, block - 0.5, 0.0)
        soft = 0.125 * block[4:5, :] * block[4:5, :]
        f, g = factors(coords, soft)
        if c_lane is not None:
            cut = slice(c_lane * TILE, (c_lane + 1) * TILE)
            source[c_step, :, cut] = g.astype(jnp.bfloat16)
            mass[c_step, :, cut] = jnp.broadcast_to(block[3:4, :], (8, TILE))
        if c_target is not None:
            target[c_target] = f.T.astype(jnp.bfloat16)
            sums[c_target] = jnp.zeros((TILE, TILE), jnp.float32)

    def own_step(j, _):
        for i in range(PER_STEP):
            c = j * PER_STEP + i
            prepare(dense[c], j, i, c, lane + c * TILE < total)
        return 0

    lax.fori_loop(0, n_steps, own_step, 0)

    def hot_step(j, _):
        for i in range(PER_STEP):
            prepare(got[j * PER_STEP + i, 8:16, :], STEPS + j, i, None, lane >= 0)
        return 0

    n_hot = jnp.where(agreed, STEPS, 0)
    lax.fori_loop(0, n_hot, hot_step, 0)
    hot_block = got[me, 8:16, :]
    prepare(hot_block, None, None, PB, lane >= 0)
    n_own = n_targets * n_steps
    n_all = n_own + n_hot

    def following(ti, sj):
        end = sj + 1 == jnp.where(ti == PB, STEPS + STEPS, n_steps)
        ti2 = jnp.where(end, ti + 1, ti)
        sj2 = jnp.where(end, 0, sj + 1)
        to_hot = end & (ti2 == n_targets) & (ti < PB)
        return (
            jnp.minimum(jnp.where(to_hot, PB, ti2), PB),
            jnp.minimum(jnp.where(to_hot, STEPS, sj2), 2 * STEPS - 1),
        )

    def distances(ti, sj, d_ref):
        d_ref[...] = jnp.dot(target[ti], source[sj], preferred_element_type=jnp.float32)

    def weigh(t, ti, sj, d_ref):
        slot = jnp.where(t < n_all, ti, PB + 1)
        for r in range(0, TILE, 16):
            value = None
            for i in range(PER_STEP):
                cut = slice(i * TILE, (i + 1) * TILE)
                m = jnp.concatenate([mass[sj, :, cut]] * 2, axis=0)
                term = lax.rsqrt(d_ref[r : r + 16, cut]) * m
                value = term if value is None else value + term
            sums[slot, r : r + 16, :] += value

    start_t = jnp.where(n_own > 0, 0, PB)
    start_s = jnp.where(n_own > 0, 0, STEPS)

    def turn(i, carry):
        ti, sj = carry
        ti2, sj2 = following(ti, sj)
        ti3, sj3 = following(ti2, sj2)
        distances(ti2, sj2, d_odd)
        weigh(2 * i, ti, sj, d_even)
        distances(ti3, sj3, d_even)
        weigh(2 * i + 1, ti2, sj2, d_odd)
        return ti3, sj3

    distances(start_t, start_s, d_even)
    lax.fori_loop(0, (n_all + 1) // 2, turn, (start_t, start_s))

    def finish(c, block):
        summed = jnp.sum(sums[c].T, axis=0, keepdims=True)
        return 2.0 * block[3:4, :] / block[4:5, :] - summed

    def own_finish(c, carry):
        block = dense[c]
        phi = finish(c, block)
        phis[pl.ds(c, 1), :] = phi
        live = lanes((1, TILE)) + c * TILE < total
        return carry + jnp.where(live, block[3:4, :] * phi, 0.0)

    carry = lax.fori_loop(0, n_targets, own_finish, jnp.zeros((1, TILE), jnp.float32))
    energy[...] = jnp.broadcast_to(0.5 * jnp.sum(carry, axis=1, keepdims=True), energy.shape)
    phi = finish(PB, hot_block)
    share = 0.5 * jnp.sum(hot_block[3:4, :] * phi, axis=1, keepdims=True)
    share = jnp.broadcast_to(share, (1, TILE))
    narrow = lanes((1, TILE))
    eight = rows((8, TILE))
    hot_phi[...] = jnp.where(
        eight == 0, phi, jnp.where(agreed, least, -1.0)
    )

    for s in range(PB):
        at = offs[s]
        q, r = at // TILE, at % TILE
        both = jnp.where(narrow >= r, phis[pl.ds(q, 1), :], phis[pl.ds(q + 1, 1), :])
        back[s, 0:1, :] = pltpu.roll(both, (TILE - r) % TILE, 1)
        back[s, 1:2, :] = share


def unpack_kernel(place, counts, owners, back, hot_phi, energy_in, out, energy):
    me = place[0]
    hot = jnp.max(hot_phi[1:2, :]).astype(jnp.int32)
    lane = lanes((1, TILE))
    out[...] = jnp.zeros(out.shape, jnp.float32)
    special = hot_phi[0:1, :]

    def group(k, carry):
        at, held = carry
        count = counts[0, k]
        q, r = at // TILE, at % TILE
        value = jnp.where(k == hot, special, back[owners[0, k], 0:1, :])
        value = jnp.where(lane < count, value, 0.0)
        rolled = pltpu.roll(value, r, 1)
        merged = jnp.where(lane < r, held, rolled)
        out[pl.ds(q, 1), :] = merged
        out[pl.ds(q + 1, 1), :] = jnp.where(lane < r, rolled, 0.0)
        after = at + count
        held = jnp.where(after // TILE == q, merged, rolled)
        return after, held

    lax.fori_loop(
        0, GROUPS, group, (jnp.int32(0), jnp.zeros((1, TILE), jnp.float32)), unroll=8
    )
    shares = jnp.sum(back[:, 1, :], axis=0, keepdims=True)
    is_owner = (hot >= 0) & (owners[0, jnp.maximum(hot, 0)] == me)
    energy[...] = jnp.where(is_owner, shares, energy_in[0:1, :])


def per_device(positions, masses, smoothing, block_lists, block_counts, group_owner):
    f32 = jnp.float32
    place = lax.axis_index("slab").astype(jnp.int32).reshape(1)
    blocks, message = pl.pallas_call(
        pack_kernel,
        out_shape=(
            jax.ShapeDtypeStruct((PB, 8, TILE), f32),
            jax.ShapeDtypeStruct((GROUPS, 16, TILE), f32),
        ),
        in_specs=[SMEM, SMEM, VMEM, VMEM, VMEM],
        out_specs=(VMEM, VMEM),
        compiler_params=params(),
        name="pack",
    )(block_counts, group_owner, positions, masses, smoothing)
    slabs = lax.axis_size(("slab", "grp"))
    up = [(i, (i + 1) % slabs) for i in range(slabs)]
    down = [(t, s) for s, t in up]
    below = lax.ppermute(blocks, ("slab", "grp"), up)
    above = lax.ppermute(blocks, ("slab", "grp"), down)
    got = lax.all_to_all(message, "slab", split_axis=0, concat_axis=0, tiled=True)
    density = pl.pallas_call(
        density_kernel,
        out_shape=jax.ShapeDtypeStruct((PB, TILE), f32),
        in_specs=[SMEM, VMEM, VMEM, VMEM],
        out_specs=VMEM,
        scratch_shapes=[
            pltpu.VMEM((3 * PB, 32, TILE), jnp.bfloat16),
            pltpu.VMEM((PB, TILE, 32), jnp.bfloat16),
            pltpu.VMEM((3 * PB, 8, TILE), f32),
            pltpu.VMEM((TILE, COLS * TILE), f32),
            pltpu.VMEM((TILE, COLS * TILE), f32),
            pltpu.VMEM((TILE, TILE), f32),
            pltpu.VMEM((TILE, TILE), f32),
        ],
        compiler_params=params(),
        cost_estimate=pl.CostEstimate(flops=10**10, bytes_accessed=10**6, transcendentals=0),
        name="density",
    )(block_lists, blocks, below, above)
    back, hot_phi, energy = pl.pallas_call(
        potential_kernel,
        out_shape=(
            jax.ShapeDtypeStruct((GROUPS, 2, TILE), f32),
            jax.ShapeDtypeStruct((8, TILE), f32),
            jax.ShapeDtypeStruct((8, TILE), f32),
        ),
        in_specs=[SMEM, SMEM, VMEM],
        out_specs=(VMEM, VMEM, VMEM),
        scratch_shapes=[
            pltpu.SMEM((PB,), jnp.int32),
            pltpu.VMEM((PB + 2 * PER_STEP, 8, TILE), f32),
            pltpu.VMEM((PB + 8, TILE), f32),
            pltpu.VMEM((2 * STEPS, 32, STEP), jnp.bfloat16),
            pltpu.VMEM((PB + 2, TILE, 32), jnp.bfloat16),
            pltpu.VMEM((2 * STEPS, 8, STEP), f32),
            pltpu.VMEM((PB + 2, TILE, TILE), f32),
            pltpu.VMEM((TILE, STEP), f32),
            pltpu.VMEM((TILE, STEP), f32),
        ],
        compiler_params=params(),
        cost_estimate=pl.CostEstimate(flops=10**10, bytes_accessed=10**6, transcendentals=0),
        name="potential",
    )(place, group_owner, got)
    returned = lax.all_to_all(back, "slab", split_axis=0, concat_axis=0, tiled=True)
    potential, energy = pl.pallas_call(
        unpack_kernel,
        out_shape=(
            jax.ShapeDtypeStruct((PB + 8, TILE), f32),
            jax.ShapeDtypeStruct((1, TILE), f32),
        ),
        in_specs=[SMEM, SMEM, SMEM, VMEM, VMEM, VMEM],
        out_specs=(VMEM, VMEM),
        compiler_params=params(),
        name="unpack",
    )(place, block_counts, group_owner, returned, hot_phi, energy)
    return (
        density.reshape(1, -1),
        potential[:PB].reshape(1, -1),
        energy[:, :1],
    )


def solution(mesh):
    placed = (
        P(("slab", "grp"), None, None),
        P(("slab", "grp"), None),
        P(("slab", "grp"), None),
        P(("slab", "grp"), None, None),
        P(("slab", "grp"), None),
        P("grp", None),
    )
    return jax.shard_map(
        per_device,
        mesh=mesh,
        in_specs=placed,
        out_specs=(P(("slab", "grp"), None), P(("slab", "grp"), None), P("grp", "slab")),
        check_vma=False,
    )
```

time: 370 us -> 102 us (0.28)
  other arithmetic: 189 us -> 0 us
  local copies, waits for them, and re-layouts: 109 us -> 1.71 us
  Pallas kernels: 0 us -> 57.9 us
  loops' own time: 32.2 us -> 0 us
  waiting for transfers between devices: 7.99 us -> 14.9 us
    reduce_sum x28 -> x0, other arithmetic: 178 us -> none  [the longest x16 131 us: row_block(): summed = jnp.sum(inverse * members[3][None, :], axis=1)]
    gather x10 -> x0, local copies, waits for them, and re-layouts: 80.5 us -> none  [the longest x1 45.5 us: per_device(): potential = jnp.where(member_of < groups_here, returned[flat_index], 0.0)]
    pallas_call x0 -> x4, Pallas kernels: none -> 57.9 us  [the longest x1 30.6 us: per_device(): pl.pallas_call(density_kernel, out_shape=jax.ShapeDtypeStruct((PB, TILE),...]
    another operation x2 -> x0, loops' own time: 32.2 us -> none  [the longest x1 31.6 us: potential_all(): return lax.map(row_block, starts).reshape(total_rows)]
    dynamic_slice x32 -> x0, local copies, waits for them, and re-layouts: 10.7 us -> none  [the longest x16 9.42 us: potential_all(): return lax.map(row_block, starts).reshape(total_rows)]
    slice x43 -> x1, local copies, waits for them, and re-layouts: 11.1 us -> 0.62 us  [per_device(): potential[:PB].reshape(1, -1)]
    select_n x13 -> x0, other arithmetic: 7.11 us -> none  [the longest x2 6.25 us: per_device(): jnp.take(particles, row_index.reshape(-1), axis=1)]
    all_to_all x2, waiting for transfers between devices: 7.98 us -> 14.9 us  [the longest x1 14.9 us: per_device(): lax.all_to_all(message, 'slab', split_axis=0, concat_axis=0, tiled=True)]
  transfers between devices with their start and end apart: 4 -> 4, of which waited for: 1 -> 1; matrix products, arithmetic and copies ran while one was open for 28% -> 0% of each run, Pallas kernels for 0% -> 53%
where the time goes in v1:
time: 102 us; the launch traced here: 101 us
  Pallas kernels  57.9 us (57%)
  starting transfers between devices  25.4 us (25%)
  waiting for transfers between devices  14.9 us (15%)
  local copies, waits for them, and re-layouts  1.71 us (2%)
    pallas_call x1, Pallas kernels, per_device(): pl.pallas_call(density_kernel, out_shape=jax.ShapeDtypeStruct((PB, TILE),...  30.6 us
    pallas_call x1, Pallas kernels, per_device(): pl.pallas_call(potential_kernel, out_shape=(jax.ShapeDtypeStruct((GROUPS,...  22.5 us
    all_to_all x1, waiting for transfers between devices, per_device(): lax.all_to_all(message, 'slab', split_axis=0, concat_axis=0, tiled=True)  14.9 us
    all_to_all x1, starting transfers between devices, per_device(): lax.all_to_all(message, 'slab', split_axis=0, concat_axis=0, tiled=True)  13.2 us
    all_to_all x1, starting transfers between devices, per_device(): lax.all_to_all(back, 'slab', split_axis=0, concat_axis=0, tiled=True)  9.23 us
    pallas_call x1, Pallas kernels, per_device(): pl.pallas_call(pack_kernel, out_shape=(jax.ShapeDtypeStruct((PB, 8, TILE)...  2.76 us
    pallas_call x1, Pallas kernels, per_device(): pl.pallas_call(unpack_kernel, out_shape=(jax.ShapeDtypeStruct((PB + 8, TI...  2.06 us
  transfers between devices with their start and end apart: 4, of which 1 were waited for; matrix products, arithmetic and copies ran while one was open for 0% of the time, Pallas kernels for 53%

profile of v1, /device:TPU:1, one launch (start us, length us, event | category | flops | bytes accessed | tf_op | source)
XLA Modules:
  0.0 100.7 jit_solution(8161784253882755186)
XLA Ops:
  0.6 0.0 copy-start.2
  0.6 0.0 copy-start.3
  0.7 0.0 copy-start
  0.7 0.0 copy-start.1
  0.7 1.0 copy.9.pos
  1.7 0.0 copy-done.2
  1.7 0.0 copy-done.3
  1.7 0.0 copy-done
  1.7 0.0 copy-done.1
  1.7 2.8 %pack.1 = (f32[64,8,128]{2,1,0:T(8,128)S(1)}, f32[64,16,128]{2,1,0:T(8,128)}) custom-call(s32[1,64]{1,0:T(1,128)S(1)} %copy-done.2, s32[1,64]{1,0:T(1,128)S(1)} %copy-done.3, f32[1,3,8192]{2,1,0:T(4,128)S(1)} %copy.9.pos, f32[1,8192]{1,0:T(1,128)S(1)} %copy-done, f32[1,8192]{1,0:T(1,128)S(1)} %copy-done.1), custom_call_target="tpu_custom_call" | custom-call | tf_op jit(solution)/shard_map/pack/pallas_call | solution.py:324
  4.5 13.2 %all-to-all-start = ((f32[64,16,128]{2,1,0:T(8,128)}), f32[64,16,128]{2,1,0:T(8,128)S(1)}, u32[]{:S(2)}, u32[]{:S(2)}) async-start(f32[64,16,128]{2,1,0:T(8,128)} %get-tuple-element.11), calls=%async_computation | async-start | bytes 1048576 | tf_op jit(solution)/shard_map/all_to_all | solution.py:340
  17.6 0.0 copy-start.4
  17.6 1.3 %collective-permute-start = (f32[64,8,128]{2,1,0:T(8,128)S(1)}, f32[64,8,128]{2,1,0:T(8,128)S(1)}, u32[]{:S(2)}, u32[]{:S(2)}) collective-permute-start(f32[64,8,128]{2,1,0:T(8,128)S(1)} %get-tuple-element.10.own), channel_id=1, source_target_pairs={{0,1},{1,2},{2,3},{3,4},{4,5},{5,6},{6,7},{7,8},{8,9},{9,10},{10,1... | collective-permute-start | bytes 786440 | tf_op jit(solution)/shard_map/ppermute | solution.py:338
  18.9 1.7 %collective-permute-start.1 = (f32[64,8,128]{2,1,0:T(8,128)S(1)}, f32[64,8,128]{2,1,0:T(8,128)S(1)}, u32[]{:S(2)}, u32[]{:S(2)}) collective-permute-start(f32[64,8,128]{2,1,0:T(8,128)S(1)} %get-tuple-element.10.own), channel_id=1, source_target_pairs={{1,0},{2,1},{3,2},{4,3},{5,4},{6,5},{7,6},{8,7},{9,8},{10,9},{11,1... | collective-permute-start | bytes 786440 | tf_op jit(solution)/shard_map/ppermute | solution.py:339
  20.7 0.0 copy-done.4
  20.7 0.1 copy.10.lists
  20.8 14.9 %all-to-all-done.got = f32[64,16,128]{2,1,0:T(8,128)S(1)} async-done(((f32[64,16,128]{2,1,0:T(8,128)}), f32[64,16,128]{2,1,0:T(8,128)S(1)}, u32[]{:S(2)}, u32[]{:S(2)}) %all-to-all-start) | async-done | bytes 524320 | tf_op jit(solution)/shard_map/all_to_all | solution.py:340
  35.6 22.5 %potential.1 = (f32[64,2,128]{2,1,0:T(2,128)}, f32[8,128]{1,0:T(8,128)S(1)}, f32[8,128]{1,0:T(8,128)S(1)}) custom-call(s32[1]{0:T(128)} %bitcast.1.place, s32[1,64]{1,0:T(1,128)S(1)} %copy-done.3, f32[64,16,128]{2,1,0:T(8,128)S(1)} %all-to-all-done.got), custom_call_target="tpu_custom_call" | custom-call | flops 10000000000 | bytes 1000000 | tf_op jit(solution)/shard_map/potential/pallas_call | solution.py:359
  58.1 9.2 %all-to-all-start.1 = ((f32[64,2,128]{2,1,0:T(2,128)}), f32[64,2,128]{2,1,0:T(2,128)S(1)}, u32[]{:S(2)}, u32[]{:S(2)}) async-start(f32[64,2,128]{2,1,0:T(2,128)} %get-tuple-element.12), calls=%async_computation.1 | async-start | bytes 131072 | tf_op jit(solution)/shard_map/all_to_all | solution.py:383
  67.4 0.0 collective-permute-done.below
  67.4 0.0 collective-permute-done.1.above
  67.4 30.6 %density.1 = f32[64,128]{1,0:T(8,128)} custom-call(s32[1,64,8]{2,1,0:T(8,128)S(1)} %copy.10.lists, f32[64,8,128]{2,1,0:T(8,128)S(1)} %get-tuple-element.10.own, f32[64,8,128]{2,1,0:T(8,128)S(1)} %collective-permute-done.below, f32[64,8,128]{2,1,0:T(8,128)S(1)} %collective-permute-done.1.above), custom_call_target="tpu_custom_call" | custom-call | flops 10000000000 | bytes 1000000 | tf_op jit(solution)/shard_map/density/pallas_call | solution.py:341
  98.0 0.0 all-to-all-done.1.back
  98.0 2.1 %unpack.1 = (f32[72,128]{1,0:T(8,128)S(1)}, f32[1,128]{1,0:T(1,128)}) custom-call(s32[1]{0:T(128)} %bitcast.1.place, s32[1,64]{1,0:T(1,128)S(1)} %copy-done.2, s32[1,64]{1,0:T(1,128)S(1)} %copy-done.3, f32[64,2,128]{2,1,0:T(2,128)S(1)} %all-to-all-done.1.back, f32[8,128]{1,0:T(8,128)S(1)} %get-tuple-element.13.hot_phi, f32[8,128]{1,0:T(8,128)S(1)} %get-tuple-element.14.energy_in), custom_call_target="tpu_custom_call" | custom-call | tf_op jit(solution)/shard_map/unpack/pallas_call | solution.py:384
  100.0 0.6 slice.6
Async XLA Ops:
  0.6 1.0 %copy-start.2 = (s32[1,64]{1,0:T(1,128)S(1)}, s32[1,64]{1,0:T(1,128)}, u32[]{:S(2)}) copy-start(s32[1,64]{1,0:T(1,128)} %counts.3) | copy-start | bytes 772
  0.6 1.0 %copy-start.3 = (s32[1,64]{1,0:T(1,128)S(1)}, s32[1,64]{1,0:T(1,128)}, u32[]{:S(2)}) copy-start(s32[1,64]{1,0:T(1,128)} %owners.5) | copy-start | bytes 772
  0.7 1.0 %copy-start = (f32[1,8192]{1,0:T(1,128)S(1)}, f32[1,8192]{1,0:T(1,128)}, u32[]{:S(2)}) copy-start(f32[1,8192]{1,0:T(1,128)} %mass.1) | copy-start | bytes 98308
  0.7 1.0 %copy-start.1 = (f32[1,8192]{1,0:T(1,128)S(1)}, f32[1,8192]{1,0:T(1,128)}, u32[]{:S(2)}) copy-start(f32[1,8192]{1,0:T(1,128)} %smooth.1) | copy-start | bytes 98308
  4.5 31.2 %all-to-all-start = ((f32[64,16,128]{2,1,0:T(8,128)}), f32[64,16,128]{2,1,0:T(8,128)S(1)}, u32[]{:S(2)}, u32[]{:S(2)}) async-start(f32[64,16,128]{2,1,0:T(8,128)} %get-tuple-element.11), calls=%async_computation | async-start | bytes 1048576 | tf_op jit(solution)/shard_map/all_to_all | solution.py:340
  17.6 3.1 %copy-start.4 = (s32[1,64,8]{1,2,0:T(8,128)S(1)}, s32[1,64,8]{1,2,0:T(8,128)}, u32[]{:S(2)}) copy-start(s32[1,64,8]{1,2,0:T(8,128)} %param.9) | copy-start | bytes 6148
  17.6 49.7 %collective-permute-start = (f32[64,8,128]{2,1,0:T(8,128)S(1)}, f32[64,8,128]{2,1,0:T(8,128)S(1)}, u32[]{:S(2)}, u32[]{:S(2)}) collective-permute-start(f32[64,8,128]{2,1,0:T(8,128)S(1)} %get-tuple-element.10.own), channel_id=1, source_target_pairs={{0,1},{1,2},{2,3},{3,4},{4,5},{5,6},{6,7},{7,8},{8,9},{9,10},{10,1... | collective-permute-start | bytes 786440 | tf_op jit(solution)/shard_map/ppermute | solution.py:338
  18.9 48.5 %collective-permute-start.1 = (f32[64,8,128]{2,1,0:T(8,128)S(1)}, f32[64,8,128]{2,1,0:T(8,128)S(1)}, u32[]{:S(2)}, u32[]{:S(2)}) collective-permute-start(f32[64,8,128]{2,1,0:T(8,128)S(1)} %get-tuple-element.10.own), channel_id=1, source_target_pairs={{1,0},{2,1},{3,2},{4,3},{5,4},{6,5},{7,6},{8,7},{9,8},{10,9},{11,1... | collective-permute-start | bytes 786440 | tf_op jit(solution)/shard_map/ppermute | solution.py:339
  58.1 39.9 %all-to-all-start.1 = ((f32[64,2,128]{2,1,0:T(2,128)}), f32[64,2,128]{2,1,0:T(2,128)S(1)}, u32[]{:S(2)}, u32[]{:S(2)}) async-start(f32[64,2,128]{2,1,0:T(2,128)} %get-tuple-element.12), calls=%async_computation.1 | async-start | bytes 131072 | tf_op jit(solution)/shard_map/all_to_all | solution.py:383

commit v2 on v1

v2 whole, which is shorter than its diff:
```python
import functools
import math

import jax
import jax.numpy as jnp
from jax import lax
from jax.experimental import pallas as pl
from jax.experimental.pallas import tpu as pltpu
from jax.sharding import PartitionSpec as P

TILE = 128
PB = 64
KX = 2
KO = 4
COLS = 2 * KX + KO
GROUPS = 64
UNITS = 16
WIDE = 256
FIRST = 32
KERNEL_NORM = 21.0 / (16.0 * math.pi)
VMEM = pl.BlockSpec(memory_space=pltpu.VMEM)
SMEM = pl.BlockSpec(memory_space=pltpu.SMEM)


def params():
    return pltpu.CompilerParams(vmem_limit_bytes=48 * 1024 * 1024)


def lanes(shape):
    return lax.broadcasted_iota(jnp.int32, shape, len(shape) - 1)


def rows(shape):
    return lax.broadcasted_iota(jnp.int32, shape, len(shape) - 2)


def split(value):
    high = value.astype(jnp.bfloat16).astype(jnp.float32)
    return high, value - high


def split3(value):
    first, rest = split(value)
    second, third = split(rest)
    return first, second, third


def place_factors(block, shift, stage, target, source):
    for kind, out in (("target", target), ("source", source)):
        if out is None:
            continue
        for c in range(0, PB, 8):
            highs, lows, norm = [], [], None
            for k in range(3):
                coord = block[c : c + 8, k, :] - 0.5
                if k == 0 and shift:
                    coord = coord + shift
                high, low = split(coord)
                highs.append(high)
                lows.append(low)
                norm = coord * coord if norm is None else norm + coord * coord
            norms = list(split3(norm))
            ones = [jnp.ones_like(norm)] * 3
            if kind == "target":
                lines = highs + highs + lows + norms + ones
            else:
                highs = [-2.0 * v for v in highs]
                lows = [-2.0 * v for v in lows]
                lines = highs + lows + highs + ones + norms
            for k, line in enumerate(lines + [jnp.zeros_like(norm)]):
                stage[c : c + 8, k, :] = line
            out[c : c + 8] = stage[c : c + 8].astype(jnp.bfloat16)


def pack_kernel(counts, owners, pos, mass, smooth, blocks, message):
    for c in range(PB):
        cut = slice(c * TILE, (c + 1) * TILE)
        blocks[c, 0:3, :] = pos[0, :, cut]
        blocks[c, 3:4, :] = mass[:, cut]
        blocks[c, 4:5, :] = smooth[:, cut]
        blocks[c, 5:8, :] = jnp.zeros((3, TILE), jnp.float32)
    lane = lanes((8, TILE))
    row = rows((8, TILE))

    def window(start):
        q = jnp.minimum(start // TILE, PB - 1)
        r = start % TILE
        both = jnp.where(lane >= r, blocks[q], blocks[jnp.minimum(q + 1, PB - 1)])
        return pltpu.roll(both, (TILE - r) % TILE, 1)

    def group(k, carry):
        start, hot, hot_start = carry
        count = counts[0, k]
        value = window(start)
        value = jnp.where((row == 3) & (lane >= count), 0.0, value)
        value = jnp.where(row == 5, count.astype(jnp.float32), value)
        place = owners[0, k]
        message[place, 0] = value[0:4]
        message[place, 1, 0:2, :] = value[4:6]
        first = (count == TILE) & (hot < 0)
        return (
            start + count,
            jnp.where(first, k, hot),
            jnp.where(first, start, hot_start),
        )

    _, hot, hot_start = lax.fori_loop(
        0, GROUPS, group, (jnp.int32(0), jnp.int32(-1), jnp.int32(0)), unroll=8
    )
    value = jnp.where(row == 5, hot.astype(jnp.float32), window(hot_start))
    for d in range(GROUPS):
        message[d, 1, 2:4, :] = value[4:6]
        message[d, 2] = value[0:4]


def contract(a, b):
    return lax.dot_general(a, b, (((0,), (0,)), ((), ())), preferred_element_type=jnp.float32)


def tall(line):
    return jnp.broadcast_to(line, (TILE, TILE)).T


def column_pass(picks, b_first, b_count, targets, own, sources, others, out, buffers, add, up):
    columns = len(picks)
    last = b_first + b_count - 1

    def distances(b, buffer):
        d_ref, wide_h, wide_m = buffer
        b = jnp.minimum(b, last)
        factor = targets[b]
        for s in range(0, columns, 2):
            pair = jnp.concatenate([sources[picks[s](b)], sources[picks[s + 1](b)]], axis=1)
            d_ref[:, s * TILE : (s + 2) * TILE] = contract(factor, pair)
        wide_h[...] = tall(own[b, 4:5, :])
        if up is not None:
            wide_m[...] = tall(own[b, 3:4, :] * (32.0 * KERNEL_NORM))

    def weigh(b, buffer):
        d_ref, wide_h, wide_m = buffer
        where = [pick(b) for pick in picks]
        hs = [others[c, 4:5, :] for c in where]
        ms = [others[c, 3:4, :] * (1.0 if up is not None else 32.0 * KERNEL_NORM) for c in where]
        total = []
        upward = [None] * columns
        for r in range(0, TILE, 8):
            part = None
            mine = wide_h[r : r + 8, :]
            for s in range(columns):
                d2 = jnp.maximum(d_ref[r : r + 8, s * TILE : (s + 1) * TILE], 1e-20)
                inverse = pl.reciprocal(mine + hs[s], approx=True)
                t = d2 * lax.rsqrt(d2) * inverse
                fall = jnp.maximum(1.0 - t, 0.0)
                fall = fall * fall
                fall = fall * fall
                shape = fall * (0.25 + t)
                if up is None:
                    value = shape * ((inverse * inverse) * (inverse * ms[s]))
                else:
                    value = shape * (inverse * inverse * inverse)
                    send = value * wide_m[r : r + 8, :]
                    upward[s] = send if upward[s] is None else upward[s] + send
                    value = value * ms[s]
                part = value if part is None else part + value
            total.append(part)
        whole = jnp.concatenate(total, axis=0)
        line = jnp.sum(whole.T, axis=0, keepdims=True)
        if up is not None:
            line = line * (32.0 * KERNEL_NORM)
            for s in range(columns):
                up[where[s]] += upward[s]
        if add:
            line = line + out[pl.ds(b, 1), :]
        out[pl.ds(b, 1), :] = line

    even, odd = buffers
    distances(jnp.int32(b_first), even)

    def turn(i, _):
        b = b_first + 2 * i
        distances(b + 1, odd)
        weigh(b, even)
        distances(b + 2, even)
        weigh(b + 1, odd)
        return 0

    lax.fori_loop(0, b_count // 2, turn, 0)


def picks_of(lists, first, count):
    return [lambda b, s=s: lists[0, b, s] for s in range(first, first + count)]


def cross_kernel(lists, own, above, out, up, target, source, over, up_sum, stage, stage_up, *scratch):
    place_factors(own, 0.0, stage, target, None)
    place_factors(above, 1.0, stage_up, None, over)
    place_factors(own, 0.0, stage, None, source)
    up_sum[...] = jnp.zeros(up_sum.shape, jnp.float32)
    buffers = (scratch[0:3], scratch[3:6])
    column_pass(
        picks_of(lists, KX + KO, KX), 0, PB, target, own, over, above, out, buffers, False, up_sum
    )
    column_pass(
        picks_of(lists, KX, KO), 0, FIRST, target, own, source, own, out, buffers, True, None
    )
    for c in range(0, PB, 8):
        total = up_sum[c : c + 8, 0, :]
        for k in range(1, 8):
            total = total + up_sum[c : c + 8, k, :]
        up[c : c + 8, :] = total


def rest_kernel(lists, own, target, source, part, below, after, out, *scratch):
    out[...] = part[...] + below[...]
    buffers = (scratch[0:3], scratch[3:6])
    column_pass(
        picks_of(lists, KX, KO), FIRST, PB - FIRST, target, own, source, own, out, buffers, True, None
    )


def potential_kernel(
    place, owners, got, after, back, hot_phi, energy, offs, dense, phis, source, target, sums, hot_sums, aims, gives
):
    me = place[0]
    lane = lanes((8, TILE))
    row = rows((8, TILE))
    labels = got[:, 1, 3, :]
    least = jnp.min(labels)
    agreed = least == jnp.max(labels)
    hot = jnp.maximum(least.astype(jnp.int32), 0)
    mine = agreed & (owners[0, hot] == me)

    at = jnp.int32(0)
    held = jnp.zeros((8, TILE), jnp.float32)
    for s in range(PB):
        q, r = at // TILE, at % TILE
        offs[s] = at
        block = jnp.concatenate([got[s, 0], got[s, 1]], axis=0)
        rolled = pltpu.roll(block, r, 1)
        merged = jnp.where(lane < r, held, rolled)
        dense[q] = merged
        dense[q + 1] = rolled
        at = at + got[s, 1, 1:2, 0:1][0, 0].astype(jnp.int32)
        held = jnp.where(at // TILE == q, merged, rolled)
    total = at
    total = jnp.where(mine, 0, total)
    n_tiles = (total + WIDE - 1) // WIDE
    n_all = n_tiles * n_tiles
    one = jnp.ones((8, TILE), jnp.float32)

    def pieces(coords, m, h, valid, aims, gives):
        norm = 0.125 * h * h
        for v in coords:
            norm = norm + v * v
        scale = 1.0 / (m * m)
        n0, n1, n2 = split3(norm)
        w0, w1, w2 = split3(scale)
        cost = scale * norm
        if valid is not None:
            cost = jnp.where(valid, cost, 1e30)
        g0, g1, g2 = split3(cost)
        parts = [split(v) for v in coords]
        sent = [split(-2.0 * scale * v) for v in coords]
        if aims is not None:
            lines = [p[0] for p in parts] * 2 + [p[1] for p in parts]
            lines += [n0, n0, n0, n1, n1, n2, one, one, one]
            for k, line in enumerate(lines):
                aims[:, k, :] = line
        if gives is not None:
            lines = [p[0] for p in sent] + [p[1] for p in sent] + [p[0] for p in sent]
            lines += [w0, w1, w2, w0, w1, w0, g0, g1, g2]
            for k, line in enumerate(lines):
                gives[:, k, :] = line

    aims[:, 16:32, :] = jnp.zeros((8, 16, TILE), jnp.float32)
    gives[:, 16:32, :] = jnp.zeros((8, 16, TILE), jnp.float32)

    def own_factors(g, _):
        at = pl.multiple_of(g * 8, 8)
        index = (at + row) * TILE + lane
        valid = index < total
        coords = [jnp.where(valid, dense[pl.ds(at, 8), k, :] - 0.5, 0.0) for k in range(3)]
        m = jnp.where(valid, dense[pl.ds(at, 8), 3, :], 1.0)
        h = jnp.where(valid, dense[pl.ds(at, 8), 4, :], 1.0)
        pieces(coords, m, h, valid, aims, gives)
        for i in range(8):
            tile = g * 4 + i // 2
            cut = slice((i % 2) * TILE, (i % 2 + 1) * TILE)
            target[tile, :, cut] = aims[i].astype(jnp.bfloat16)
            source[tile, cut, :] = gives[i].T.astype(jnp.bfloat16)
            if i % 2 == 0:
                sums[tile] = jnp.zeros((8, WIDE), jnp.float32)
        return 0

    lax.fori_loop(0, (total + 8 * TILE - 1) // (8 * TILE), own_factors, 0)

    def added(d):
        parts = [None] * 4
        for n in range(d.shape[0] // 8):
            term = lax.rsqrt(d[8 * n : 8 * n + 8, :])
            parts[n % 4] = term if parts[n % 4] is None else parts[n % 4] + term
        return (parts[0] + parts[1]) + (parts[2] + parts[3])

    def turn(i, carry):
        ti, sj = carry
        units = []
        for u in range(UNITS):
            units.append((jnp.where(i * UNITS + u < n_all, ti, PB // 2), sj))
            end = sj + 1 >= n_tiles
            ti, sj = jnp.where(end, ti + 1, ti), jnp.where(end, 0, sj + 1)
        for slot, other in units:
            d = jnp.dot(source[other], target[slot], preferred_element_type=jnp.float32)
            sums[slot] += added(d)
        return ti, sj

    lax.fori_loop(0, (n_all + UNITS - 1) // UNITS, turn, (jnp.int32(0), jnp.int32(0)))

    hot_block = jnp.concatenate([got[me, 2], got[me, 1, 2:4, :], got[me, 1, 2:4, :]], axis=0)
    hot_sums[...] = jnp.zeros((8, TILE), jnp.float32)

    @pl.when(agreed)
    def _():
        for g in range(8):
            cut = slice(g * 8, g * 8 + 8)
            coords = [got[cut, 2, k, :] - 0.5 for k in range(3)]
            pieces(coords, got[cut, 2, 3, :], got[cut, 1, 2, :], None, None, gives)
            for i in range(8):
                half = slice((i % 2) * TILE, (i % 2 + 1) * TILE)
                source[g * 4 + i // 2, half, :] = gives[i].T.astype(jnp.bfloat16)
        coords = [got[me, 2, k : k + 1, :] - 0.5 for k in range(3)]
        coords = [jnp.broadcast_to(v, (8, TILE)) for v in coords]
        m = jnp.broadcast_to(hot_block[3:4], (8, TILE))
        h = jnp.broadcast_to(hot_block[4:5], (8, TILE))
        pieces(coords, m, h, None, aims, None)
        aim = aims[0].astype(jnp.bfloat16)
        for j in range(PB // 2):
            hot_sums[...] += added(jnp.dot(source[j], aim, preferred_element_type=jnp.float32))

    def finish(block, summed):
        return 2.0 * block[3:4, :] / block[4:5, :] - jnp.sum(summed, axis=0, keepdims=True)

    def own_finish(t, carry):
        for half in range(2):
            c = 2 * t + half
            block = dense[c]
            phi = finish(block, sums[t, :, half * TILE : (half + 1) * TILE])
            phis[pl.ds(c, 1), :] = phi
            live = lanes((1, TILE)) + c * TILE < total
            carry = carry + jnp.where(live, block[3:4, :] * phi, 0.0)
        return carry

    carry = lax.fori_loop(0, n_tiles, own_finish, jnp.zeros((1, TILE), jnp.float32))
    energy[...] = jnp.broadcast_to(0.5 * jnp.sum(carry, axis=1, keepdims=True), energy.shape)
    phi = finish(hot_block, hot_sums[...])
    share = 0.5 * jnp.sum(hot_block[3:4, :] * phi, axis=1, keepdims=True)
    share = jnp.broadcast_to(share, (1, TILE))
    narrow = lanes((1, TILE))
    eight = rows((8, TILE))
    hot_phi[...] = jnp.where(eight == 0, phi, jnp.where(agreed, least, -1.0))

    for s in range(PB):
        at = offs[s]
        q, r = at // TILE, at % TILE
        both = jnp.where(narrow >= r, phis[pl.ds(q, 1), :], phis[pl.ds(q + 1, 1), :])
        back[s, 0:1, :] = pltpu.roll(both, (TILE - r) % TILE, 1)
        back[s, 1:2, :] = share


def unpack_kernel(place, counts, owners, back, hot_phi, energy_in, result, energy, out):
    me = place[0]
    hot = jnp.max(hot_phi[1:2, :]).astype(jnp.int32)
    lane = lanes((1, TILE))
    out[...] = jnp.zeros(out.shape, jnp.float32)
    special = hot_phi[0:1, :]

    def group(k, carry):
        at, held = carry
        count = counts[0, k]
        q, r = at // TILE, at % TILE
        value = jnp.where(k == hot, special, back[owners[0, k], 0:1, :])
        value = jnp.where(lane < count, value, 0.0)
        rolled = pltpu.roll(value, r, 1)
        merged = jnp.where(lane < r, held, rolled)
        out[pl.ds(q, 1), :] = merged
        out[pl.ds(q + 1, 1), :] = jnp.where(lane < r, rolled, 0.0)
        after = at + count
        held = jnp.where(after // TILE == q, merged, rolled)
        return after, held

    lax.fori_loop(
        0, GROUPS, group, (jnp.int32(0), jnp.zeros((1, TILE), jnp.float32)), unroll=8
    )
    result[...] = out[0:PB, :]
    shares = jnp.sum(back[:, 1, :], axis=0, keepdims=True)
    is_owner = (hot >= 0) & (owners[0, jnp.maximum(hot, 0)] == me)
    energy[...] = jnp.where(is_owner, shares, energy_in[0:1, :])


def per_device(positions, masses, smoothing, block_lists, block_counts, group_owner):
    f32 = jnp.float32
    place = lax.axis_index("slab").astype(jnp.int32).reshape(1)
    blocks, message = pl.pallas_call(
        pack_kernel,
        out_shape=(
            jax.ShapeDtypeStruct((PB, 8, TILE), f32),
            jax.ShapeDtypeStruct((GROUPS, 3, 4, TILE), f32),
        ),
        in_specs=[SMEM, SMEM, VMEM, VMEM, VMEM],
        out_specs=(VMEM, VMEM),
        compiler_params=params(),
        name="pack",
    )(block_counts, group_owner, positions, masses, smoothing)
    slabs = lax.axis_size(("slab", "grp"))
    up = [(i, (i + 1) % slabs) for i in range(slabs)]
    down = [(t, s) for s, t in up]
    above = lax.ppermute(blocks, ("slab", "grp"), down)
    got = lax.all_to_all(message, "slab", split_axis=0, concat_axis=0, tiled=True)
    buffers = [
        pltpu.VMEM((TILE, KO * TILE), f32),
        pltpu.VMEM((TILE, TILE), f32),
        pltpu.VMEM((TILE, TILE), f32),
    ] * 2
    lines = jax.ShapeDtypeStruct((PB, TILE), f32)
    pieces = jax.ShapeDtypeStruct((PB, 16, TILE), jnp.bfloat16)
    cost = pl.CostEstimate(flops=10**10, bytes_accessed=10**6, transcendentals=0)
    part, upward, target, source = pl.pallas_call(
        cross_kernel,
        out_shape=(lines, lines, pieces, pieces),
        in_specs=[SMEM, VMEM, VMEM],
        out_specs=(VMEM, VMEM, VMEM, VMEM),
        scratch_shapes=[
            pltpu.VMEM((PB, 16, TILE), jnp.bfloat16),
            pltpu.VMEM((PB, 8, TILE), f32),
            pltpu.VMEM((PB, 16, TILE), f32),
            pltpu.VMEM((PB, 16, TILE), f32),
            *buffers,
        ],
        compiler_params=params(),
        cost_estimate=cost,
        name="cross",
    )(block_lists, blocks, above)
    from_below = lax.ppermute(upward, ("slab", "grp"), up)
    back, hot_phi, energy = pl.pallas_call(
        potential_kernel,
        out_shape=(
            jax.ShapeDtypeStruct((GROUPS, 2, TILE), f32),
            jax.ShapeDtypeStruct((8, TILE), f32),
            jax.ShapeDtypeStruct((8, TILE), f32),
        ),
        in_specs=[SMEM, SMEM, VMEM, pl.BlockSpec(memory_space=pl.ANY)],
        out_specs=(VMEM, VMEM, VMEM),
        scratch_shapes=[
            pltpu.SMEM((PB,), jnp.int32),
            pltpu.VMEM((PB + 8, 8, TILE), f32),
            pltpu.VMEM((PB + 8, TILE), f32),
            pltpu.VMEM((PB // 2, WIDE, 32), jnp.bfloat16),
            pltpu.VMEM((PB // 2 + 1, 32, WIDE), jnp.bfloat16),
            pltpu.VMEM((PB // 2 + 1, 8, WIDE), f32),
            pltpu.VMEM((8, TILE), f32),
            pltpu.VMEM((8, 32, TILE), f32),
            pltpu.VMEM((8, 32, TILE), f32),
        ],
        compiler_params=params(),
        cost_estimate=cost,
        name="potential",
    )(place, group_owner, got, part)
    density = pl.pallas_call(
        rest_kernel,
        out_shape=lines,
        in_specs=[SMEM, VMEM, VMEM, VMEM, VMEM, VMEM, pl.BlockSpec(memory_space=pl.ANY)],
        out_specs=VMEM,
        scratch_shapes=buffers,
        compiler_params=params(),
        cost_estimate=cost,
        name="rest",
    )(block_lists, blocks, target, source, part, from_below, hot_phi)
    returned = lax.all_to_all(back, "slab", split_axis=0, concat_axis=0, tiled=True)
    potential, energy = pl.pallas_call(
        unpack_kernel,
        out_shape=(
            jax.ShapeDtypeStruct((PB, TILE), f32),
            jax.ShapeDtypeStruct((1, TILE), f32),
        ),
        in_specs=[SMEM, SMEM, SMEM, VMEM, VMEM, VMEM],
        out_specs=(VMEM, VMEM),
        scratch_shapes=[pltpu.VMEM((PB + 8, TILE), f32)],
        compiler_params=params(),
        name="unpack",
    )(place, block_counts, group_owner, returned, hot_phi, energy)
    return (
        density.reshape(1, -1),
        potential.reshape(1, -1),
        energy[:, :1],
    )


def solution(mesh):
    placed = (
        P(("slab", "grp"), None, None),
        P(("slab", "grp"), None),
        P(("slab", "grp"), None),
        P(("slab", "grp"), None, None),
        P(("slab", "grp"), None),
        P("grp", None),
    )
    return jax.shard_map(
        per_device,
        mesh=mesh,
        in_specs=placed,
        out_specs=(P(("slab", "grp"), None), P(("slab", "grp"), None), P("grp", "slab")),
        check_vma=False,
    )
```

time: 102 us -> 75.2 us (0.74)
  waiting for transfers between devices: 14.9 us -> 1.41 us
  Pallas kernels: 57.9 us -> 45 us
    all_to_all x1, waiting for transfers between devices: 14.9 us -> 0.01 us  [per_device(): lax.all_to_all(message, 'slab', split_axis=0, concat_axis=0, tiled=True)]
    pallas_call x1, Pallas kernels: 22.5 us -> 11.4 us  [per_device(): pl.pallas_call(potential_kernel, out_shape=(jax.ShapeDtypeStruct((GROUPS,...]
    ppermute x1, starting transfers between devices: 1.75 us -> 3.87 us  [per_device(): above = lax.ppermute(blocks, ('slab', 'grp'), down)]
    pallas_call x2 -> x3, Pallas kernels: 32.6 us -> 31 us  [the longest x1 20.1 us: per_device(): pl.pallas_call(cross_kernel, out_shape=(lines, lines, pieces, pieces), in...]
    all_to_all x1, waiting for transfers between devices: 0.01 us -> 1.4 us  [per_device(): lax.all_to_all(back, 'slab', split_axis=0, concat_axis=0, tiled=True)]
    all_to_all x1, starting transfers between devices: 13.2 us -> 11.8 us  [per_device(): lax.all_to_all(message, 'slab', split_axis=0, concat_axis=0, tiled=True)]
    ppermute x1, starting transfers between devices: 1.3 us -> 0.09 us  [per_device(): from_below = lax.ppermute(upward, ('slab', 'grp'), up)]
  transfers between devices with their start and end apart: 4 -> 4, of which waited for: 1 -> 1; matrix products, arithmetic and copies ran while one was open for 0% -> 0% of each run, Pallas kernels for 53% -> 54%
where the time goes in v2:
time: 75.2 us; the launch traced here: 74.8 us
  Pallas kernels  45 us (60%)
  starting transfers between devices  25.8 us (34%)
  local copies, waits for them, and re-layouts  1.76 us (2%)
  waiting for transfers between devices  1.41 us (2%)
  between operations  0.76 us (1%)
    pallas_call x1, Pallas kernels, per_device(): pl.pallas_call(cross_kernel, out_shape=(lines, lines, pieces, pieces), in...  20.1 us
    all_to_all x1, starting transfers between devices, per_device(): lax.all_to_all(message, 'slab', split_axis=0, concat_axis=0, tiled=True)  11.8 us
    pallas_call x1, Pallas kernels, per_device(): pl.pallas_call(potential_kernel, out_shape=(jax.ShapeDtypeStruct((GROUPS,...  11.4 us
    all_to_all x1, starting transfers between devices, per_device(): lax.all_to_all(back, 'slab', split_axis=0, concat_axis=0, tiled=True)  10.1 us
    pallas_call x1, Pallas kernels, per_device(): pl.pallas_call(rest_kernel, out_shape=lines, in_specs=[SMEM, VMEM, VMEM,...  8.67 us
    ppermute x1, starting transfers between devices, per_device(): above = lax.ppermute(blocks, ('slab', 'grp'), down)  3.87 us
    pallas_call x1, Pallas kernels, per_device(): pl.pallas_call(pack_kernel, out_shape=(jax.ShapeDtypeStruct((PB, 8, TILE)...  2.7 us
    pallas_call x1, Pallas kernels, per_device(): pl.pallas_call(unpack_kernel, out_shape=(jax.ShapeDtypeStruct((PB, TILE),...  2.14 us
  transfers between devices with their start and end apart: 4, of which 1 were waited for; matrix products, arithmetic and copies ran while one was open for 0% of the time, Pallas kernels for 54%

profile of v2, /device:TPU:1, one launch (start us, length us, event | category | flops | bytes accessed | tf_op | source)
XLA Modules:
  0.0 74.8 jit_solution(553787984369845421)
XLA Ops:
  0.6 0.0 copy-start.3
  0.6 0.0 copy-start.2
  0.7 0.0 copy-start.1
  0.7 0.0 copy-start
  0.7 1.0 %copy.9.pos = f32[1,3,8192]{2,1,0:T(4,128)S(1)} copy(f32[1,3,8192]{2,0,1:T(1,128)} %param.6) | data formatting | bytes 196608 | tf_op args[0]
  1.7 0.0 copy-done.3
  1.7 0.0 copy-done.2
  1.7 0.0 copy-done.1
  1.7 0.0 copy-done
  1.7 2.7 %pack.1 = (f32[64,8,128]{2,1,0:T(8,128)S(1)}, f32[64,3,4,128]{3,2,1,0:T(4,128)}) custom-call(s32[1,64]{1,0:T(1,128)S(1)} %copy-done.2, s32[1,64]{1,0:T(1,128)S(1)} %copy-done.3, f32[1,3,8192]{2,1,0:T(4,128)S(1)} %copy.9.pos, f32[1,8192]{1,0:T(1,128)S(1)} %copy-done, f32[1,8192]{1,0:T(1,128)S(1)} %copy-done.1), custom_call_target="tpu_custom_call" | custom-call | tf_op jit(solution)/shard_map/pack/pallas_call | solution.py:402
  4.4 3.9 %collective-permute-start = (f32[64,8,128]{2,1,0:T(8,128)S(1)}, f32[64,8,128]{2,1,0:T(8,128)S(1)}, u32[]{:S(2)}, u32[]{:S(2)}) collective-permute-start(f32[64,8,128]{2,1,0:T(8,128)S(1)} %get-tuple-element.14.own), channel_id=1, source_target_pairs={{1,0},{2,1},{3,2},{4,3},{5,4},{6,5},{7,6},{8,7},{9,8},{10,9},{11,1... | collective-permute-start | bytes 786440 | tf_op jit(solution)/shard_map/ppermute | solution.py:416
  8.3 11.8 %all-to-all-start = ((f32[64,3,4,128]{3,2,1,0:T(4,128)}), f32[64,3,4,128]{3,2,1,0:T(4,128)S(1)}, u32[]{:S(2)}, u32[]{:S(2)}) async-start(f32[64,3,4,128]{3,2,1,0:T(4,128)} %get-tuple-element.19), calls=%async_computation | async-start | bytes 786432 | tf_op jit(solution)/shard_map/all_to_all | solution.py:417
  20.0 0.0 copy-start.4
  20.1 0.7 copy-done.4
  20.7 0.1 copy.11.lists
  20.8 0.0 collective-permute-done.above
  20.8 20.1 %cross.1 = (f32[64,128]{1,0:T(8,128)S(1)}, f32[64,128]{1,0:T(8,128)S(1)}, bf16[64,16,128]{2,1,0:T(8,128)(2,1)S(1)}, bf16[64,16,128]{2,1,0:T(8,128)(2,1)S(1)}) custom-call(s32[1,64,8]{2,1,0:T(8,128)S(1)} %copy.11.lists, f32[64,8,128]{2,1,0:T(8,128)S(1)} %get-tuple-element.14.own, f32[64,8,128]{2,1,0:T(8,128)S(1)} %collective-permute-done.above), custom_call_target="tpu_custom_call" | custom-call | flops 10000000000 | bytes 1000000 | tf_op jit(solution)/shard_map/cross/pallas_call | solution.py:426
  41.0 0.1 collective-permute-start.1
  41.1 0.0 all-to-all-done.got
  41.1 11.4 %potential.1 = (f32[64,2,128]{2,1,0:T(2,128)}, f32[8,128]{1,0:T(8,128)S(1)}, f32[8,128]{1,0:T(8,128)S(1)}) custom-call(s32[1]{0:T(128)} %bitcast.place, s32[1,64]{1,0:T(1,128)S(1)} %copy-done.3, f32[64,3,4,128]{3,2,1,0:T(4,128)S(1)} %all-to-all-done.got, f32[64,128]{1,0:T(8,128)S(1)} %get-tuple-element.17.after.part), custom_call_target="tpu_custom_call" | custom-call | flops 10000000000 | bytes 1000000 | tf_op jit(solution)/shard_map/potential/pallas_call | solution.py:443
  52.5 10.1 %all-to-all-start.1 = ((f32[64,2,128]{2,1,0:T(2,128)}), f32[64,2,128]{2,1,0:T(2,128)S(1)}, u32[]{:S(2)}, u32[]{:S(2)}) async-start(f32[64,2,128]{2,1,0:T(2,128)} %get-tuple-element.21), calls=%async_computation.1 | async-start | bytes 131072 | tf_op jit(solution)/shard_map/all_to_all | solution.py:477
  62.5 0.0 collective-permute-done.1.below
  62.5 8.7 %rest.1 = f32[64,128]{1,0:T(8,128)} custom-call(s32[1,64,8]{2,1,0:T(8,128)S(1)} %copy.11.lists, f32[64,8,128]{2,1,0:T(8,128)S(1)} %get-tuple-element.14.own, bf16[64,16,128]{2,1,0:T(8,128)(2,1)S(1)} %get-tuple-element.15.target, bf16[64,16,128]{2,1,0:T(8,128)(2,1)S(1)} %get-tuple-element.16.source, f32[64,128]{1,0:T(8,128)S(1)} %get-tuple-element.17.after.part, ...), custom_call_target="tpu_custom_call" | custom-call | flops 10000000000 | bytes 1000000 | tf_op jit(solution)/shard_map/rest/pallas_call | solution.py:467
  71.2 1.4 %all-to-all-done.1.back = f32[64,2,128]{2,1,0:T(2,128)S(1)} async-done(((f32[64,2,128]{2,1,0:T(2,128)}), f32[64,2,128]{2,1,0:T(2,128)S(1)}, u32[]{:S(2)}, u32[]{:S(2)}) %all-to-all-start.1) | async-done | bytes 65568 | tf_op jit(solution)/shard_map/all_to_all | solution.py:477
  72.6 2.1 %unpack.1 = (f32[64,128]{1,0:T(8,128)}, f32[1,128]{1,0:T(1,128)}) custom-call(s32[1]{0:T(128)} %bitcast.place, s32[1,64]{1,0:T(1,128)S(1)} %copy-done.2, s32[1,64]{1,0:T(1,128)S(1)} %copy-done.3, f32[64,2,128]{2,1,0:T(2,128)S(1)} %all-to-all-done.1.back, f32[8,128]{1,0:T(8,128)S(1)} %get-tuple-element.20.after.hot_phi, f32[8,128]{1,0:T(8,128)S(1)} %get-tuple-element.22.energy_in), custom_call_target="tpu_custom_call" | custom-call | tf_op jit(solution)/shard_map/unpack/pallas_call | solution.py:478
Async XLA Ops:
  0.6 1.0 %copy-start.3 = (s32[1,64]{1,0:T(1,128)S(1)}, s32[1,64]{1,0:T(1,128)}, u32[]{:S(2)}) copy-start(s32[1,64]{1,0:T(1,128)} %owners.5) | copy-start | bytes 772
  0.6 1.0 %copy-start.2 = (s32[1,64]{1,0:T(1,128)S(1)}, s32[1,64]{1,0:T(1,128)}, u32[]{:S(2)}) copy-start(s32[1,64]{1,0:T(1,128)} %counts.3) | copy-start | bytes 772
  0.7 1.0 %copy-start.1 = (f32[1,8192]{1,0:T(1,128)S(1)}, f32[1,8192]{1,0:T(1,128)}, u32[]{:S(2)}) copy-start(f32[1,8192]{1,0:T(1,128)} %smooth.1) | copy-start | bytes 98308
  0.7 1.0 %copy-start = (f32[1,8192]{1,0:T(1,128)S(1)}, f32[1,8192]{1,0:T(1,128)}, u32[]{:S(2)}) copy-start(f32[1,8192]{1,0:T(1,128)} %mass.1) | copy-start | bytes 98308
  4.4 16.4 %collective-permute-start = (f32[64,8,128]{2,1,0:T(8,128)S(1)}, f32[64,8,128]{2,1,0:T(8,128)S(1)}, u32[]{:S(2)}, u32[]{:S(2)}) collective-permute-start(f32[64,8,128]{2,1,0:T(8,128)S(1)} %get-tuple-element.14.own), channel_id=1, source_target_pairs={{1,0},{2,1},{3,2},{4,3},{5,4},{6,5},{7,6},{8,7},{9,8},{10,9},{11,1... | collective-permute-start | bytes 786440 | tf_op jit(solution)/shard_map/ppermute | solution.py:416
  8.3 32.8 %all-to-all-start = ((f32[64,3,4,128]{3,2,1,0:T(4,128)}), f32[64,3,4,128]{3,2,1,0:T(4,128)S(1)}, u32[]{:S(2)}, u32[]{:S(2)}) async-start(f32[64,3,4,128]{3,2,1,0:T(4,128)} %get-tuple-element.19), calls=%async_computation | async-start | bytes 786432 | tf_op jit(solution)/shard_map/all_to_all | solution.py:417
  20.0 0.7 copy-start.4
  41.0 21.6 %collective-permute-start.1 = (f32[64,128]{1,0:T(8,128)S(1)}, f32[64,128]{1,0:T(8,128)S(1)}, u32[]{:S(2)}, u32[]{:S(2)}) collective-permute-start(f32[64,128]{1,0:T(8,128)S(1)} %get-tuple-element.18), channel_id=1, source_target_pairs={{0,1},{1,2},{2,3},{3,4},{4,5},{5,6},{6,7},{7,8},{8,9},{9,10},{10,1... | collective-permute-start | bytes 98312 | tf_op jit(solution)/shard_map/ppermute | solution.py:442
  52.5 20.2 %all-to-all-start.1 = ((f32[64,2,128]{2,1,0:T(2,128)}), f32[64,2,128]{2,1,0:T(2,128)S(1)}, u32[]{:S(2)}, u32[]{:S(2)}) async-start(f32[64,2,128]{2,1,0:T(2,128)} %get-tuple-element.21), calls=%async_computation.1 | async-start | bytes 131072 | tf_op jit(solution)/shard_map/all_to_all | solution.py:477

commit v3 on v2

--- a/solution.py
+++ b/solution.py
@@ -16,14 +16,16 @@
 GROUPS = 64
 UNITS = 16
 WIDE = 256
-FIRST = 32
+FIRST = 42
+CROSS_UNROLL = 16
+OWN_UNROLL = 14
 KERNEL_NORM = 21.0 / (16.0 * math.pi)
 VMEM = pl.BlockSpec(memory_space=pltpu.VMEM)
 SMEM = pl.BlockSpec(memory_space=pltpu.SMEM)
 
 
-def params():
-    return pltpu.CompilerParams(vmem_limit_bytes=48 * 1024 * 1024)
+def params(size=32):
+    return pltpu.CompilerParams(vmem_limit_bytes=size * 1024 * 1024)
 
 
 def lanes(shape):
@@ -73,12 +75,10 @@
 
 
 def pack_kernel(counts, owners, pos, mass, smooth, blocks, message):
-    for c in range(PB):
-        cut = slice(c * TILE, (c + 1) * TILE)
-        blocks[c, 0:3, :] = pos[0, :, cut]
-        blocks[c, 3:4, :] = mass[:, cut]
-        blocks[c, 4:5, :] = smooth[:, cut]
-        blocks[c, 5:8, :] = jnp.zeros((3, TILE), jnp.float32)
+    for k, part in enumerate([pos[0], pos[1], pos[2], mass[...], smooth[...]]):
+        blocks[:, k, :] = part
+    for k in range(5, 8):
+        blocks[:, k, :] = jnp.zeros((PB, TILE), jnp.float32)
     lane = lanes((8, TILE))
     row = rows((8, TILE))
 
@@ -93,7 +93,8 @@
         count = counts[0, k]
         value = window(start)
         value = jnp.where((row == 3) & (lane >= count), 0.0, value)
-        value = jnp.where(row == 5, count.astype(jnp.float32), value)
+        note = jnp.where(lane == 0, count, k).astype(jnp.float32)
+        value = jnp.where(row == 5, note, value)
         place = owners[0, k]
         message[place, 0] = value[0:4]
         message[place, 1, 0:2, :] = value[4:6]
@@ -133,8 +134,6 @@
             pair = jnp.concatenate([sources[picks[s](b)], sources[picks[s + 1](b)]], axis=1)
             d_ref[:, s * TILE : (s + 2) * TILE] = contract(factor, pair)
         wide_h[...] = tall(own[b, 4:5, :])
-        if up is not None:
-            wide_m[...] = tall(own[b, 3:4, :] * (32.0 * KERNEL_NORM))
 
     def weigh(b, buffer):
         d_ref, wide_h, wide_m = buffer
@@ -187,27 +186,116 @@
     lax.fori_loop(0, b_count // 2, turn, 0)
 
 
+def weight(d2, reach):
+    d2 = jnp.maximum(d2, 1e-20)
+    inverse = pl.reciprocal(reach, approx=True)
+    t = d2 * lax.rsqrt(d2) * inverse
+    fall = jnp.maximum(1.0 - t, 0.0)
+    fall = fall * fall
+    return (fall * fall) * (0.25 + t), inverse
+
+
+def place_tall(block, stage, lines, wide):
+    zero = jnp.zeros((8, TILE), jnp.float32)
+    for c in range(0, PB, 8):
+        h = split3(block[c : c + 8, 4, :])
+        m = split3(block[c : c + 8, 3, :] * (32.0 * KERNEL_NORM))
+        for k, line in enumerate([*h, *m] + [zero] * 10):
+            stage[c : c + 8, k, :] = line
+        lines[c : c + 8] = stage[c : c + 8].astype(jnp.bfloat16)
+    row = rows((16, 2 * TILE))
+    lane = lanes((16, 2 * TILE))
+    choose = jnp.where((row // 3) == (lane // TILE), 1.0, 0.0).astype(jnp.bfloat16)
+
+    def step(i, _):
+        for g in range(16):
+            wide[16 * i + g] = contract(lines[16 * i + g], choose)
+        return 0
+
+    lax.fori_loop(0, PB // 16, step, 0)
+
+
+def cross_pass(lists, own, above, target, over, wide, out, up_sum):
+    def turn(i, _):
+        for g in range(CROSS_UNROLL):
+            b = i * CROSS_UNROLL + g
+            where = [lists[0, s, b] for s in range(KX)]
+            pair = jnp.concatenate([over[c] for c in where], axis=1)
+            d = contract(target[b], pair)
+            hs = [above[c, 4:5, :] for c in where]
+            ms = [above[c, 3:4, :] * (32.0 * KERNEL_NORM) for c in where]
+            upward = [None] * KX
+            total = []
+            for r in range(0, TILE, 8):
+                part = None
+                for s in range(KX):
+                    shape, inverse = weight(
+                        d[r : r + 8, s * TILE : (s + 1) * TILE], wide[b, r : r + 8, 0:TILE] + hs[s]
+                    )
+                    value = shape * (inverse * inverse * inverse)
+                    send = value * wide[b, r : r + 8, TILE : 2 * TILE]
+                    upward[s] = send if upward[s] is None else upward[s] + send
+                    value = value * ms[s]
+                    part = value if part is None else part + value
+                total.append(part)
+            whole = jnp.concatenate(total, axis=0)
+            out[pl.ds(b, 1), :] = jnp.sum(whole.T, axis=0, keepdims=True)
+            for s in range(KX):
+                up_sum[where[s]] += upward[s]
+        return 0
+
+    lax.fori_loop(0, PB // CROSS_UNROLL, turn, 0)
+
+
+def own_pass(lists, own, target, source, wide, sums):
+    def turn(i, _):
+        for g in range(OWN_UNROLL):
+            b = i * OWN_UNROLL + g
+            where = [lists[0, KX + s, b] for s in range(KO)]
+            d = contract(jnp.concatenate([source[c] for c in where], axis=1), target[b])
+            mine = own[b, 4:5, :]
+            total = [None] * 4
+            for s in range(KO):
+                for r in range(0, TILE, 8):
+                    shape, inverse = weight(
+                        d[s * TILE + r : s * TILE + r + 8, :], wide[where[s], r : r + 8, 0:TILE] + mine
+                    )
+                    scale = (inverse * inverse) * (inverse * wide[where[s], r : r + 8, TILE : 2 * TILE])
+                    total[s] = shape * scale if total[s] is None else total[s] + shape * scale
+            sums[b] = (total[0] + total[1]) + (total[2] + total[3])
+        return 0
+
+    lax.fori_loop(0, FIRST // OWN_UNROLL, turn, 0)
+
+
+def folded(block, c):
+    total = block[c : c + 8, 0, :]
+    for k in range(1, 8):
+        total = total + block[c : c + 8, k, :]
+    return total
+
+
 def picks_of(lists, first, count):
-    return [lambda b, s=s: lists[0, b, s] for s in range(first, first + count)]
-
-
-def cross_kernel(lists, own, above, out, up, target, source, over, up_sum, stage, stage_up, *scratch):
-    place_factors(own, 0.0, stage, target, None)
-    place_factors(above, 1.0, stage_up, None, over)
-    place_factors(own, 0.0, stage, None, source)
+    return [lambda b, s=s: lists[0, s, b] for s in range(first, first + count)]
+
+
+def cross_kernel(
+    listed, own, above, out, up, target, source, over, up_sum, stage, stage_up, lines, wide, sums, lists, ready
+):
+    fetch = pltpu.make_async_copy(listed, lists, ready)
+    fetch.start()
+    place_tall(own, stage, lines, wide)
+    place_factors(own, 0.0, stage_up, target, None)
+    place_factors(above, -1.0, stage, None, over)
+    place_factors(own, 0.0, stage_up, None, source)
     up_sum[...] = jnp.zeros(up_sum.shape, jnp.float32)
-    buffers = (scratch[0:3], scratch[3:6])
-    column_pass(
-        picks_of(lists, KX + KO, KX), 0, PB, target, own, over, above, out, buffers, False, up_sum
-    )
-    column_pass(
-        picks_of(lists, KX, KO), 0, FIRST, target, own, source, own, out, buffers, True, None
-    )
+    sums[...] = jnp.zeros(sums.shape, jnp.float32)
+    fetch.wait()
+    cross_pass(lists, own, above, target, over, wide, out, up_sum)
+    own_pass(lists, own, target, source, wide, sums)
     for c in range(0, PB, 8):
-        total = up_sum[c : c + 8, 0, :]
-        for k in range(1, 8):
-            total = total + up_sum[c : c + 8, k, :]
-        up[c : c + 8, :] = total
+        up[c : c + 8, :] = folded(up_sum, c)
+        out[c : c + 8, :] += folded(sums, c)
 
 
 def rest_kernel(lists, own, target, source, part, below, after, out, *scratch):
@@ -219,7 +307,7 @@
 
 
 def potential_kernel(
-    place, owners, got, after, back, hot_phi, energy, offs, dense, phis, source, target, sums, hot_sums, aims, gives
+    place, got, after, back, hot_phi, energy, offs, dense, phis, source, target, sums, hot_sums, aims, gives
 ):
     me = place[0]
     lane = lanes((8, TILE))
@@ -227,8 +315,7 @@
     labels = got[:, 1, 3, :]
     least = jnp.min(labels)
     agreed = least == jnp.max(labels)
-    hot = jnp.maximum(least.astype(jnp.int32), 0)
-    mine = agreed & (owners[0, hot] == me)
+    mine = agreed & (least == jnp.max(got[0, 1, 1:2, 1:TILE]))
 
     at = jnp.int32(0)
     held = jnp.zeros((8, TILE), jnp.float32)
@@ -316,7 +403,7 @@
     lax.fori_loop(0, (n_all + UNITS - 1) // UNITS, turn, (jnp.int32(0), jnp.int32(0)))
 
     hot_block = jnp.concatenate([got[me, 2], got[me, 1, 2:4, :], got[me, 1, 2:4, :]], axis=0)
-    hot_sums[...] = jnp.zeros((8, TILE), jnp.float32)
+    hot_sums[...] = jnp.zeros((TILE, TILE), jnp.float32)
 
     @pl.when(agreed)
     def _():
@@ -326,15 +413,20 @@
             pieces(coords, got[cut, 2, 3, :], got[cut, 1, 2, :], None, None, gives)
             for i in range(8):
                 half = slice((i % 2) * TILE, (i % 2 + 1) * TILE)
-                source[g * 4 + i // 2, half, :] = gives[i].T.astype(jnp.bfloat16)
+                target[g * 4 + i // 2, :, half] = gives[i].astype(jnp.bfloat16)
         coords = [got[me, 2, k : k + 1, :] - 0.5 for k in range(3)]
         coords = [jnp.broadcast_to(v, (8, TILE)) for v in coords]
         m = jnp.broadcast_to(hot_block[3:4], (8, TILE))
         h = jnp.broadcast_to(hot_block[4:5], (8, TILE))
         pieces(coords, m, h, None, aims, None)
-        aim = aims[0].astype(jnp.bfloat16)
-        for j in range(PB // 2):
-            hot_sums[...] += added(jnp.dot(source[j], aim, preferred_element_type=jnp.float32))
+        aim = aims[0].T.astype(jnp.bfloat16)
+        for j in range(0, PB // 2, 4):
+            total = None
+            for u in range(4):
+                d = lax.rsqrt(jnp.dot(aim, target[j + u], preferred_element_type=jnp.float32))
+                both = d[:, 0:TILE] + d[:, TILE:WIDE]
+                total = both if total is None else total + both
+            hot_sums[...] += total
 
     def finish(block, summed):
         return 2.0 * block[3:4, :] / block[4:5, :] - jnp.sum(summed, axis=0, keepdims=True)
@@ -351,7 +443,7 @@
 
     carry = lax.fori_loop(0, n_tiles, own_finish, jnp.zeros((1, TILE), jnp.float32))
     energy[...] = jnp.broadcast_to(0.5 * jnp.sum(carry, axis=1, keepdims=True), energy.shape)
-    phi = finish(hot_block, hot_sums[...])
+    phi = finish(hot_block, hot_sums[...].T)
     share = 0.5 * jnp.sum(hot_block[3:4, :] * phi, axis=1, keepdims=True)
     share = jnp.broadcast_to(share, (1, TILE))
     narrow = lanes((1, TILE))
@@ -399,6 +491,7 @@
 def per_device(positions, masses, smoothing, block_lists, block_counts, group_owner):
     f32 = jnp.float32
     place = lax.axis_index("slab").astype(jnp.int32).reshape(1)
+    lists = block_lists.transpose(0, 2, 1)
     blocks, message = pl.pallas_call(
         pack_kernel,
         out_shape=(
@@ -407,13 +500,19 @@
         ),
         in_specs=[SMEM, SMEM, VMEM, VMEM, VMEM],
         out_specs=(VMEM, VMEM),
-        compiler_params=params(),
+        compiler_params=params(60),
         name="pack",
-    )(block_counts, group_owner, positions, masses, smoothing)
+    )(
+        block_counts,
+        group_owner,
+        positions.transpose(1, 0, 2).reshape(3, PB, TILE),
+        masses.reshape(PB, TILE),
+        smoothing.reshape(PB, TILE),
+    )
     slabs = lax.axis_size(("slab", "grp"))
     up = [(i, (i + 1) % slabs) for i in range(slabs)]
     down = [(t, s) for s, t in up]
-    above = lax.ppermute(blocks, ("slab", "grp"), down)
+    above = lax.ppermute(blocks, ("slab", "grp"), up)
     got = lax.all_to_all(message, "slab", split_axis=0, concat_axis=0, tiled=True)
     buffers = [
         pltpu.VMEM((TILE, KO * TILE), f32),
@@ -426,20 +525,24 @@
     part, upward, target, source = pl.pallas_call(
         cross_kernel,
         out_shape=(lines, lines, pieces, pieces),
-        in_specs=[SMEM, VMEM, VMEM],
+        in_specs=[pl.BlockSpec(memory_space=pl.ANY), VMEM, VMEM],
         out_specs=(VMEM, VMEM, VMEM, VMEM),
         scratch_shapes=[
             pltpu.VMEM((PB, 16, TILE), jnp.bfloat16),
             pltpu.VMEM((PB, 8, TILE), f32),
             pltpu.VMEM((PB, 16, TILE), f32),
             pltpu.VMEM((PB, 16, TILE), f32),
-            *buffers,
+            pltpu.VMEM((PB, 16, TILE), jnp.bfloat16),
+            pltpu.VMEM((PB, TILE, 2 * TILE), f32),
+            pltpu.VMEM((PB, 8, TILE), f32),
+            pltpu.SMEM((1, COLS, PB), jnp.int32),
+            pltpu.SemaphoreType.DMA,
         ],
         compiler_params=params(),
         cost_estimate=cost,
         name="cross",
-    )(block_lists, blocks, above)
-    from_below = lax.ppermute(upward, ("slab", "grp"), up)
+    )(lists, blocks, above)
+    from_below = lax.ppermute(upward, ("slab", "grp"), down)
     back, hot_phi, energy = pl.pallas_call(
         potential_kernel,
         out_shape=(
@@ -447,7 +550,7 @@
             jax.ShapeDtypeStruct((8, TILE), f32),
             jax.ShapeDtypeStruct((8, TILE), f32),
         ),
-        in_specs=[SMEM, SMEM, VMEM, pl.BlockSpec(memory_space=pl.ANY)],
+        in_specs=[SMEM, VMEM, pl.BlockSpec(memory_space=pl.ANY)],
         out_specs=(VMEM, VMEM, VMEM),
         scratch_shapes=[
             pltpu.SMEM((PB,), jnp.int32),
@@ -456,14 +559,14 @@
             pltpu.VMEM((PB // 2, WIDE, 32), jnp.bfloat16),
             pltpu.VMEM((PB // 2 + 1, 32, WIDE), jnp.bfloat16),
             pltpu.VMEM((PB // 2 + 1, 8, WIDE), f32),
-            pltpu.VMEM((8, TILE), f32),
+            pltpu.VMEM((TILE, TILE), f32),
             pltpu.VMEM((8, 32, TILE), f32),
             pltpu.VMEM((8, 32, TILE), f32),
         ],
         compiler_params=params(),
         cost_estimate=cost,
         name="potential",
-    )(place, group_owner, got, part)
+    )(place, got, part)
     density = pl.pallas_call(
         rest_kernel,
         out_shape=lines,
@@ -473,7 +576,7 @@
         compiler_params=params(),
         cost_estimate=cost,
         name="rest",
-    )(block_lists, blocks, target, source, part, from_below, hot_phi)
+    )(lists, blocks, target, source, part, from_below, hot_phi)
     returned = lax.all_to_all(back, "slab", split_axis=0, concat_axis=0, tiled=True)
     potential, energy = pl.pallas_call(
         unpack_kernel,

time: 75.2 us -> 72.5 us (0.964)
  Pallas kernels: 45 us -> 38.3 us
  starting transfers between devices: 25.8 us -> 28.5 us
  waiting for transfers between devices: 1.41 us -> 3.98 us
  local copies, waits for them, and re-layouts: 1.76 us -> 0.67 us
    pallas_call x1, Pallas kernels: 8.67 us -> 6.11 us  [per_device(): pl.pallas_call(rest_kernel, out_shape=lines, in_specs=[SMEM, VMEM, VMEM,...]
    all_to_all x1, waiting for transfers between devices: 1.4 us -> 3.97 us  [per_device(): lax.all_to_all(back, 'slab', split_axis=0, concat_axis=0, tiled=True)]
    pallas_call x1, Pallas kernels: 20.1 us -> 17.6 us  [per_device(): pl.pallas_call(cross_kernel, out_shape=(lines, lines, pieces, pieces), in...]
    pallas_call x1, Pallas kernels: 11.4 us -> 9.31 us  [per_device(): pl.pallas_call(potential_kernel, out_shape=(jax.ShapeDtypeStruct((GROUPS,...]
    all_to_all x1, starting transfers between devices: 10.1 us -> 11.4 us  [per_device(): lax.all_to_all(back, 'slab', split_axis=0, concat_axis=0, tiled=True)]
    unnamed x12 -> x8, local copies, waits for them, and re-layouts: 1.76 us -> 0.67 us
    all_to_all x1, starting transfers between devices: 11.8 us -> 12.7 us  [per_device(): lax.all_to_all(message, 'slab', split_axis=0, concat_axis=0, tiled=True)]
  transfers between devices with their start and end apart: 4 -> 4, of which waited for: 1 -> 1; matrix products, arithmetic and copies ran while one was open for 0% -> 0% of each run, Pallas kernels for 54% -> 46%
where the time goes in v3:
time: 72.5 us; the launch traced here: 72.2 us
  Pallas kernels  38.3 us (53%)
  starting transfers between devices  28.5 us (39%)
  waiting for transfers between devices  3.98 us (5%)
    pallas_call x1, Pallas kernels, per_device(): pl.pallas_call(cross_kernel, out_shape=(lines, lines, pieces, pieces), in...  17.6 us
    all_to_all x1, starting transfers between devices, per_device(): lax.all_to_all(message, 'slab', split_axis=0, concat_axis=0, tiled=True)  12.7 us
    all_to_all x1, starting transfers between devices, per_device(): lax.all_to_all(back, 'slab', split_axis=0, concat_axis=0, tiled=True)  11.4 us
    pallas_call x1, Pallas kernels, per_device(): pl.pallas_call(potential_kernel, out_shape=(jax.ShapeDtypeStruct((GROUPS,...  9.31 us
    pallas_call x1, Pallas kernels, per_device(): pl.pallas_call(rest_kernel, out_shape=lines, in_specs=[SMEM, VMEM, VMEM,...  6.11 us
    all_to_all x1, waiting for transfers between devices, per_device(): lax.all_to_all(back, 'slab', split_axis=0, concat_axis=0, tiled=True)  3.97 us
    pallas_call x1, Pallas kernels, per_device(): pl.pallas_call(pack_kernel, out_shape=(jax.ShapeDtypeStruct((PB, 8, TILE)...  3.15 us
    ppermute x1, starting transfers between devices, per_device(): from_below = lax.ppermute(upward, ('slab', 'grp'), down)  2.33 us
  transfers between devices with their start and end apart: 4, of which 1 were waited for; matrix products, arithmetic and copies ran while one was open for 0% of the time, Pallas kernels for 46%

profile of v3, /device:TPU:1, one launch (start us, length us, event | category | flops | bytes accessed | tf_op | source)
XLA Modules:
  0.0 72.2 jit_solution(9145350188184358228)
XLA Ops:
  0.6 3.1 %pack.1 = (f32[64,8,128]{2,1,0:T(8,128)}, f32[64,3,4,128]{3,2,1,0:T(4,128)}) custom-call(s32[1,64]{1,0:T(1,128)} %counts.3, s32[1,64]{1,0:T(1,128)} %owners.3, f32[3,64,128]{2,1,0:T(8,128)} %bitcast.10, f32[64,128]{1,0:T(8,128)} %bitcast.11, f32[64,128]{1,0:T(8,128)} %bitcast.12), custom_call_target="tpu_custom_call" | custom-call | tf_op jit(solution)/shard_map/pack/pallas_call | solution.py:495
  3.8 2.0 %collective-permute-start = (f32[64,8,128]{2,1,0:T(8,128)}, f32[64,8,128]{2,1,0:T(8,128)S(1)}, u32[]{:S(2)}, u32[]{:S(2)}) collective-permute-start(f32[64,8,128]{2,1,0:T(8,128)} %get-tuple-element.14.own), channel_id=1, source_target_pairs={{0,1},{1,2},{2,3},{3,4},{4,5},{5,6},{6,7},{7,8},{8,9},{9,10},{10,1... | collective-permute-start | bytes 786440 | tf_op jit(solution)/shard_map/ppermute | solution.py:515
  5.8 0.0 copy-start.2
  5.8 12.7 %all-to-all-start = ((f32[64,3,4,128]{3,2,1,0:T(4,128)}), f32[64,3,4,128]{3,2,1,0:T(4,128)S(1)}, u32[]{:S(2)}, u32[]{:S(2)}) async-start(f32[64,3,4,128]{3,2,1,0:T(4,128)} %get-tuple-element.19), calls=%async_computation | async-start | bytes 786432 | tf_op jit(solution)/shard_map/all_to_all | solution.py:516
  18.6 0.0 copy-start.3
  18.6 0.0 collective-permute-done.above
  18.6 0.0 copy-done.2
  18.6 0.7 copy-done.3
  19.3 17.6 %cross.1 = (f32[64,128]{1,0:T(8,128)S(1)}, f32[64,128]{1,0:T(8,128)S(1)}, bf16[64,16,128]{2,1,0:T(8,128)(2,1)S(1)}, bf16[64,16,128]{2,1,0:T(8,128)(2,1)S(1)}) custom-call(s32[1,8,64]{2,1,0:T(8,128)S(1)} %bitcast.8, f32[64,8,128]{2,1,0:T(8,128)S(1)} %copy-done.2, f32[64,8,128]{2,1,0:T(8,128)S(1)} %collective-permute-done.above), custom_call_target="tpu_custom_call" | custom-call | flops 10000000000 | bytes 1000000 | tf_op jit(solution)/shard_map/cross/pallas_call | solution.py:525
  36.9 2.3 %collective-permute-start.1 = (f32[64,128]{1,0:T(8,128)S(1)}, f32[64,128]{1,0:T(8,128)S(1)}, u32[]{:S(2)}, u32[]{:S(2)}) collective-permute-start(f32[64,128]{1,0:T(8,128)S(1)} %get-tuple-element.18), channel_id=1, source_target_pairs={{1,0},{2,1},{3,2},{4,3},{5,4},{6,5},{7,6},{8,7},{9,8},{10,9},{11,1... | collective-permute-start | bytes 98312 | tf_op jit(solution)/shard_map/ppermute | solution.py:545
  39.2 0.0 all-to-all-done.got
  39.2 9.3 %potential.1 = (f32[64,2,128]{2,1,0:T(2,128)}, f32[8,128]{1,0:T(8,128)S(1)}, f32[8,128]{1,0:T(8,128)S(1)}) custom-call(s32[1]{0:T(128)} %bitcast.4.place, f32[64,3,4,128]{3,2,1,0:T(4,128)S(1)} %all-to-all-done.got, f32[64,128]{1,0:T(8,128)S(1)} %get-tuple-element.17.after.part), custom_call_target="tpu_custom_call" | custom-call | flops 10000000000 | bytes 1000000 | tf_op jit(solution)/shard_map/potential/pallas_call | solution.py:546
  48.6 11.4 %all-to-all-start.1 = ((f32[64,2,128]{2,1,0:T(2,128)}), f32[64,2,128]{2,1,0:T(2,128)S(1)}, u32[]{:S(2)}, u32[]{:S(2)}) async-start(f32[64,2,128]{2,1,0:T(2,128)} %get-tuple-element.21), calls=%async_computation.1 | async-start | bytes 131072 | tf_op jit(solution)/shard_map/all_to_all | solution.py:580
  60.0 0.0 collective-permute-done.1.below
  60.0 6.1 %rest.1 = f32[64,128]{1,0:T(8,128)} custom-call(s32[1,8,64]{2,1,0:T(8,128)S(1)} %bitcast.9, f32[64,8,128]{2,1,0:T(8,128)S(1)} %copy-done.2, bf16[64,16,128]{2,1,0:T(8,128)(2,1)S(1)} %get-tuple-element.15.target, bf16[64,16,128]{2,1,0:T(8,128)(2,1)S(1)} %get-tuple-element.16.source, f32[64,128]{1,0:T(8,128)S(1)} %get-tuple-element.17.after.part, ...), custom_call_target="tpu_custom_call" | custom-call | flops 10000000000 | bytes 1000000 | tf_op jit(solution)/shard_map/rest/pallas_call | solution.py:570
  66.1 0.0 copy-start
  66.1 0.0 copy-start.1
  66.1 4.0 %all-to-all-done.1.back = f32[64,2,128]{2,1,0:T(2,128)S(1)} async-done(((f32[64,2,128]{2,1,0:T(2,128)}), f32[64,2,128]{2,1,0:T(2,128)S(1)}, u32[]{:S(2)}, u32[]{:S(2)}) %all-to-all-start.1) | async-done | bytes 65568 | tf_op jit(solution)/shard_map/all_to_all | solution.py:580
  70.1 0.0 copy-done
  70.1 0.0 copy-done.1
  70.1 2.1 %unpack.1 = (f32[64,128]{1,0:T(8,128)}, f32[1,128]{1,0:T(1,128)}) custom-call(s32[1]{0:T(128)} %bitcast.4.place, s32[1,64]{1,0:T(1,128)S(1)} %copy-done, s32[1,64]{1,0:T(1,128)S(1)} %copy-done.1, f32[64,2,128]{2,1,0:T(2,128)S(1)} %all-to-all-done.1.back, f32[8,128]{1,0:T(8,128)S(1)} %get-tuple-element.20.after.hot_phi, f32[8,128]{1,0:T(8,128)S(1)} %get-tuple-element.22.energy_in), custom_call_target="tpu_custom_call" | custom-call | tf_op jit(solution)/shard_map/unpack/pallas_call | solution.py:581
Async XLA Ops:
  3.8 14.8 %collective-permute-start = (f32[64,8,128]{2,1,0:T(8,128)}, f32[64,8,128]{2,1,0:T(8,128)S(1)}, u32[]{:S(2)}, u32[]{:S(2)}) collective-permute-start(f32[64,8,128]{2,1,0:T(8,128)} %get-tuple-element.14.own), channel_id=1, source_target_pairs={{0,1},{1,2},{2,3},{3,4},{4,5},{5,6},{6,7},{7,8},{8,9},{9,10},{10,1... | collective-permute-start | bytes 786440 | tf_op jit(solution)/shard_map/ppermute | solution.py:515
  5.8 12.8 %copy-start.2 = (f32[64,8,128]{2,1,0:T(8,128)S(1)}, f32[64,8,128]{2,1,0:T(8,128)}, u32[]{:S(2)}) copy-start(f32[64,8,128]{2,1,0:T(8,128)} %get-tuple-element.14.own) | copy-start | bytes 786436
  5.8 33.4 %all-to-all-start = ((f32[64,3,4,128]{3,2,1,0:T(4,128)}), f32[64,3,4,128]{3,2,1,0:T(4,128)S(1)}, u32[]{:S(2)}, u32[]{:S(2)}) async-start(f32[64,3,4,128]{3,2,1,0:T(4,128)} %get-tuple-element.19), calls=%async_computation | async-start | bytes 786432 | tf_op jit(solution)/shard_map/all_to_all | solution.py:516
  18.6 0.7 copy-start.3
  36.9 23.1 %collective-permute-start.1 = (f32[64,128]{1,0:T(8,128)S(1)}, f32[64,128]{1,0:T(8,128)S(1)}, u32[]{:S(2)}, u32[]{:S(2)}) collective-permute-start(f32[64,128]{1,0:T(8,128)S(1)} %get-tuple-element.18), channel_id=1, source_target_pairs={{1,0},{2,1},{3,2},{4,3},{5,4},{6,5},{7,6},{8,7},{9,8},{10,9},{11,1... | collective-permute-start | bytes 98312 | tf_op jit(solution)/shard_map/ppermute | solution.py:545
  48.6 21.5 %all-to-all-start.1 = ((f32[64,2,128]{2,1,0:T(2,128)}), f32[64,2,128]{2,1,0:T(2,128)S(1)}, u32[]{:S(2)}, u32[]{:S(2)}) async-start(f32[64,2,128]{2,1,0:T(2,128)} %get-tuple-element.21), calls=%async_computation.1 | async-start | bytes 131072 | tf_op jit(solution)/shard_map/all_to_all | solution.py:580
  66.1 4.0 %copy-start = (s32[1,64]{1,0:T(1,128)S(1)}, s32[1,64]{1,0:T(1,128)}, u32[]{:S(2)}) copy-start(s32[1,64]{1,0:T(1,128)} %counts.3) | copy-start | bytes 772
  66.1 4.0 %copy-start.1 = (s32[1,64]{1,0:T(1,128)S(1)}, s32[1,64]{1,0:T(1,128)}, u32[]{:S(2)}) copy-start(s32[1,64]{1,0:T(1,128)} %owners.3) | copy-start | bytes 772

commit v4 on v3

--- a/solution.py
+++ b/solution.py
@@ -16,9 +16,10 @@
 GROUPS = 64
 UNITS = 16
 WIDE = 256
-FIRST = 42
-CROSS_UNROLL = 16
-OWN_UNROLL = 14
+FIRST = 32
+CROSS_UNROLL = 32
+OWN_UNROLL = 16
+REST_UNROLL = 16
 KERNEL_NORM = 21.0 / (16.0 * math.pi)
 VMEM = pl.BlockSpec(memory_space=pltpu.VMEM)
 SMEM = pl.BlockSpec(memory_space=pltpu.SMEM)
@@ -118,74 +119,6 @@
     return lax.dot_general(a, b, (((0,), (0,)), ((), ())), preferred_element_type=jnp.float32)
 
 
-def tall(line):
-    return jnp.broadcast_to(line, (TILE, TILE)).T
-
-
-def column_pass(picks, b_first, b_count, targets, own, sources, others, out, buffers, add, up):
-    columns = len(picks)
-    last = b_first + b_count - 1
-
-    def distances(b, buffer):
-        d_ref, wide_h, wide_m = buffer
-        b = jnp.minimum(b, last)
-        factor = targets[b]
-        for s in range(0, columns, 2):
-            pair = jnp.concatenate([sources[picks[s](b)], sources[picks[s + 1](b)]], axis=1)
-            d_ref[:, s * TILE : (s + 2) * TILE] = contract(factor, pair)
-        wide_h[...] = tall(own[b, 4:5, :])
-
-    def weigh(b, buffer):
-        d_ref, wide_h, wide_m = buffer
-        where = [pick(b) for pick in picks]
-        hs = [others[c, 4:5, :] for c in where]
-        ms = [others[c, 3:4, :] * (1.0 if up is not None else 32.0 * KERNEL_NORM) for c in where]
-        total = []
-        upward = [None] * columns
-        for r in range(0, TILE, 8):
-            part = None
-            mine = wide_h[r : r + 8, :]
-            for s in range(columns):
-                d2 = jnp.maximum(d_ref[r : r + 8, s * TILE : (s + 1) * TILE], 1e-20)
-                inverse = pl.reciprocal(mine + hs[s], approx=True)
-                t = d2 * lax.rsqrt(d2) * inverse
-                fall = jnp.maximum(1.0 - t, 0.0)
-                fall = fall * fall
-                fall = fall * fall
-                shape = fall * (0.25 + t)
-                if up is None:
-                    value = shape * ((inverse * inverse) * (inverse * ms[s]))
-                else:
-                    value = shape * (inverse * inverse * inverse)
-                    send = value * wide_m[r : r + 8, :]
-                    upward[s] = send if upward[s] is None else upward[s] + send
-                    value = value * ms[s]
-                part = value if part is None else part + value
-            total.append(part)
-        whole = jnp.concatenate(total, axis=0)
-        line = jnp.sum(whole.T, axis=0, keepdims=True)
-        if up is not None:
-            line = line * (32.0 * KERNEL_NORM)
-            for s in range(columns):
-                up[where[s]] += upward[s]
-        if add:
-            line = line + out[pl.ds(b, 1), :]
-        out[pl.ds(b, 1), :] = line
-
-    even, odd = buffers
-    distances(jnp.int32(b_first), even)
-
-    def turn(i, _):
-        b = b_first + 2 * i
-        distances(b + 1, odd)
-        weigh(b, even)
-        distances(b + 2, even)
-        weigh(b + 1, odd)
-        return 0
-
-    lax.fori_loop(0, b_count // 2, turn, 0)
-
-
 def weight(d2, reach):
     d2 = jnp.maximum(d2, 1e-20)
     inverse = pl.reciprocal(reach, approx=True)
@@ -195,7 +128,7 @@
     return (fall * fall) * (0.25 + t), inverse
 
 
-def place_tall(block, stage, lines, wide):
+def place_lines(block, stage, lines):
     zero = jnp.zeros((8, TILE), jnp.float32)
     for c in range(0, PB, 8):
         h = split3(block[c : c + 8, 4, :])
@@ -203,25 +136,49 @@
         for k, line in enumerate([*h, *m] + [zero] * 10):
             stage[c : c + 8, k, :] = line
         lines[c : c + 8] = stage[c : c + 8].astype(jnp.bfloat16)
+
+
+def place_scaled(block, stage, sources, targets):
+    zero = jnp.zeros((8, TILE), jnp.float32)
+    one = jnp.ones((8, TILE), jnp.float32)
+    for c in range(0, PB, 8):
+        cut = slice(c, c + 8)
+        coords = [block[cut, k, :] - 0.5 for k in range(3)]
+        h = block[cut, 4, :]
+        root = jnp.exp(jnp.log(block[cut, 3, :] * (32.0 * KERNEL_NORM)) * (-1.0 / 3.0))
+        scale = root * root
+        norm = coords[0] * coords[0] + coords[1] * coords[1] + coords[2] * coords[2]
+        n0, n1, n2 = split3(norm)
+        s0, s1, s2 = split3(scale)
+        c0, c1, c2 = split3(root)
+        h0, h1, h2 = split3(h)
+        parts = [split(v) for v in coords]
+        sent = [split(-2.0 * scale * v) for v in coords]
+        high, low = [p[0] for p in parts], [p[1] for p in parts]
+        give = [p[0] for p in sent] + [p[1] for p in sent] + [p[0] for p in sent]
+        give += [s0, s1, s2, s0, s1, s0, *split3(scale * norm)]
+        give += [c0, c1, c2, c0, c1, c0, *split3(root * h)]
+        aim = high + high + low + [n0, n0, n0, n1, n1, n2, one, one, one] + [zero] * 14
+        reach = [zero] * 18 + [h0, h0, h0, h1, h1, h2, one, one, one] + [zero] * 5
+        give += [zero] * 5
+        for lines, out in ((give, sources.at[cut]), (aim, targets.at[cut, :, 0:TILE]), (reach, targets.at[cut, :, TILE:])):
+            for k, line in enumerate(lines):
+                stage[cut, k, :] = line
+            out[...] = stage[cut].astype(jnp.bfloat16)
+
+
+def cross_pass(lists, above, target, over, lines, out, up_sum):
     row = rows((16, 2 * TILE))
     lane = lanes((16, 2 * TILE))
     choose = jnp.where((row // 3) == (lane // TILE), 1.0, 0.0).astype(jnp.bfloat16)
 
-    def step(i, _):
-        for g in range(16):
-            wide[16 * i + g] = contract(lines[16 * i + g], choose)
-        return 0
-
-    lax.fori_loop(0, PB // 16, step, 0)
-
-
-def cross_pass(lists, own, above, target, over, wide, out, up_sum):
     def turn(i, _):
         for g in range(CROSS_UNROLL):
             b = i * CROSS_UNROLL + g
             where = [lists[0, s, b] for s in range(KX)]
             pair = jnp.concatenate([over[c] for c in where], axis=1)
             d = contract(target[b], pair)
+            wide = contract(lines[b], choose)
             hs = [above[c, 4:5, :] for c in where]
             ms = [above[c, 3:4, :] * (32.0 * KERNEL_NORM) for c in where]
             upward = [None] * KX
@@ -230,10 +187,10 @@
                 part = None
                 for s in range(KX):
                     shape, inverse = weight(
-                        d[r : r + 8, s * TILE : (s + 1) * TILE], wide[b, r : r + 8, 0:TILE] + hs[s]
+                        d[r : r + 8, s * TILE : (s + 1) * TILE], wide[r : r + 8, 0:TILE] + hs[s]
                     )
                     value = shape * (inverse * inverse * inverse)
-                    send = value * wide[b, r : r + 8, TILE : 2 * TILE]
+                    send = value * wide[r : r + 8, TILE : 2 * TILE]
                     upward[s] = send if upward[s] is None else upward[s] + send
                     value = value * ms[s]
                     part = value if part is None else part + value
@@ -247,25 +204,22 @@
     lax.fori_loop(0, PB // CROSS_UNROLL, turn, 0)
 
 
-def own_pass(lists, own, target, source, wide, sums):
+def own_pass(lists, first, count, unroll, targets, sources, sums):
     def turn(i, _):
-        for g in range(OWN_UNROLL):
-            b = i * OWN_UNROLL + g
+        for g in range(unroll):
+            b = first + i * unroll + g
             where = [lists[0, KX + s, b] for s in range(KO)]
-            d = contract(jnp.concatenate([source[c] for c in where], axis=1), target[b])
-            mine = own[b, 4:5, :]
+            d = contract(jnp.concatenate([sources[c] for c in where], axis=1), targets[b])
             total = [None] * 4
-            for s in range(KO):
-                for r in range(0, TILE, 8):
-                    shape, inverse = weight(
-                        d[s * TILE + r : s * TILE + r + 8, :], wide[where[s], r : r + 8, 0:TILE] + mine
-                    )
-                    scale = (inverse * inverse) * (inverse * wide[where[s], r : r + 8, TILE : 2 * TILE])
-                    total[s] = shape * scale if total[s] is None else total[s] + shape * scale
+            for n in range(KO * TILE // 8):
+                cut = slice(8 * n, 8 * n + 8)
+                shape, inverse = weight(d[cut, 0:TILE], d[cut, TILE : 2 * TILE])
+                value = shape * (inverse * inverse * inverse)
+                total[n % 4] = value if total[n % 4] is None else total[n % 4] + value
             sums[b] = (total[0] + total[1]) + (total[2] + total[3])
         return 0
 
-    lax.fori_loop(0, FIRST // OWN_UNROLL, turn, 0)
+    lax.fori_loop(0, count // unroll, turn, 0)
 
 
 def folded(block, c):
@@ -275,35 +229,31 @@
     return total
 
 
-def picks_of(lists, first, count):
-    return [lambda b, s=s: lists[0, s, b] for s in range(first, first + count)]
-
-
 def cross_kernel(
-    listed, own, above, out, up, target, source, over, up_sum, stage, stage_up, lines, wide, sums, lists, ready
+    listed, own, above, out, up, sources, targets, target, over, up_sum, stage, stage_up, wider, lines, sums, lists, ready
 ):
     fetch = pltpu.make_async_copy(listed, lists, ready)
     fetch.start()
-    place_tall(own, stage, lines, wide)
+    place_lines(own, stage, lines)
     place_factors(own, 0.0, stage_up, target, None)
     place_factors(above, -1.0, stage, None, over)
-    place_factors(own, 0.0, stage_up, None, source)
+    place_scaled(own, wider, sources, targets)
     up_sum[...] = jnp.zeros(up_sum.shape, jnp.float32)
     sums[...] = jnp.zeros(sums.shape, jnp.float32)
     fetch.wait()
-    cross_pass(lists, own, above, target, over, wide, out, up_sum)
-    own_pass(lists, own, target, source, wide, sums)
+    cross_pass(lists, above, target, over, lines, out, up_sum)
+    own_pass(lists, 0, FIRST, OWN_UNROLL, targets, sources, sums)
     for c in range(0, PB, 8):
         up[c : c + 8, :] = folded(up_sum, c)
         out[c : c + 8, :] += folded(sums, c)
 
 
-def rest_kernel(lists, own, target, source, part, below, after, out, *scratch):
-    out[...] = part[...] + below[...]
-    buffers = (scratch[0:3], scratch[3:6])
-    column_pass(
-        picks_of(lists, KX, KO), FIRST, PB - FIRST, target, own, source, own, out, buffers, True, None
-    )
+def rest_kernel(lists, sources, targets, part, below, after, out, sums):
+    sums[...] = jnp.zeros(sums.shape, jnp.float32)
+    own_pass(lists, FIRST, PB - FIRST, REST_UNROLL, targets, sources, sums)
+    for c in range(0, PB, 8):
+        cut = slice(c, c + 8)
+        out[cut, :] = part[cut, :] + below[cut, :] + folded(sums, c)
 
 
 def potential_kernel(
@@ -514,26 +464,26 @@
     down = [(t, s) for s, t in up]
     above = lax.ppermute(blocks, ("slab", "grp"), up)
     got = lax.all_to_all(message, "slab", split_axis=0, concat_axis=0, tiled=True)
-    buffers = [
-        pltpu.VMEM((TILE, KO * TILE), f32),
-        pltpu.VMEM((TILE, TILE), f32),
-        pltpu.VMEM((TILE, TILE), f32),
-    ] * 2
     lines = jax.ShapeDtypeStruct((PB, TILE), f32)
-    pieces = jax.ShapeDtypeStruct((PB, 16, TILE), jnp.bfloat16)
     cost = pl.CostEstimate(flops=10**10, bytes_accessed=10**6, transcendentals=0)
-    part, upward, target, source = pl.pallas_call(
+    part, upward, sources, targets = pl.pallas_call(
         cross_kernel,
-        out_shape=(lines, lines, pieces, pieces),
+        out_shape=(
+            lines,
+            lines,
+            jax.ShapeDtypeStruct((PB, 32, TILE), jnp.bfloat16),
+            jax.ShapeDtypeStruct((PB, 32, 2 * TILE), jnp.bfloat16),
+        ),
         in_specs=[pl.BlockSpec(memory_space=pl.ANY), VMEM, VMEM],
         out_specs=(VMEM, VMEM, VMEM, VMEM),
         scratch_shapes=[
             pltpu.VMEM((PB, 16, TILE), jnp.bfloat16),
+            pltpu.VMEM((PB, 16, TILE), jnp.bfloat16),
             pltpu.VMEM((PB, 8, TILE), f32),
             pltpu.VMEM((PB, 16, TILE), f32),
             pltpu.VMEM((PB, 16, TILE), f32),
+            pltpu.VMEM((PB, 32, TILE), f32),
             pltpu.VMEM((PB, 16, TILE), jnp.bfloat16),
-            pltpu.VMEM((PB, TILE, 2 * TILE), f32),
             pltpu.VMEM((PB, 8, TILE), f32),
             pltpu.SMEM((1, COLS, PB), jnp.int32),
             pltpu.SemaphoreType.DMA,
@@ -570,13 +520,13 @@
     density = pl.pallas_call(
         rest_kernel,
         out_shape=lines,
-        in_specs=[SMEM, VMEM, VMEM, VMEM, VMEM, VMEM, pl.BlockSpec(memory_space=pl.ANY)],
+        in_specs=[SMEM, VMEM, VMEM, VMEM, VMEM, pl.BlockSpec(memory_space=pl.ANY)],
         out_specs=VMEM,
-        scratch_shapes=buffers,
+        scratch_shapes=[pltpu.VMEM((PB, 8, TILE), f32)],
         compiler_params=params(),
         cost_estimate=cost,
         name="rest",
-    )(lists, blocks, target, source, part, from_below, hot_phi)
+    )(lists, sources, targets, part, from_below, hot_phi)
     returned = lax.all_to_all(back, "slab", split_axis=0, concat_axis=0, tiled=True)
     potential, energy = pl.pallas_call(
         unpack_kernel,

time: 72.5 us -> 69.7 us (0.961)
  Pallas kernels: 38.3 us -> 36.8 us
  starting transfers between devices: 28.5 us -> 27.3 us
    pallas_call x1, Pallas kernels: 17.6 us -> 15.1 us  [per_device(): pl.pallas_call(cross_kernel, out_shape=(lines, lines, jax.ShapeDtypeStruc...]
    all_to_all x1, starting transfers between devices: 11.4 us -> 10 us  [per_device(): lax.all_to_all(back, 'slab', split_axis=0, concat_axis=0, tiled=True)]
where the time goes in v4:
time: 69.7 us; the launch traced here: 69 us
  Pallas kernels  36.8 us (53%)
  starting transfers between devices  27.3 us (39%)
  waiting for transfers between devices  3.57 us (5%)
  between operations  0.7 us (1%)
    pallas_call x1, Pallas kernels, per_device(): pl.pallas_call(cross_kernel, out_shape=(lines, lines, jax.ShapeDtypeStruc...  15.1 us
    all_to_all x1, starting transfers between devices, per_device(): lax.all_to_all(message, 'slab', split_axis=0, concat_axis=0, tiled=True)  12.7 us
    all_to_all x1, starting transfers between devices, per_device(): lax.all_to_all(back, 'slab', split_axis=0, concat_axis=0, tiled=True)  10 us
    pallas_call x1, Pallas kernels, per_device(): pl.pallas_call(potential_kernel, out_shape=(jax.ShapeDtypeStruct((GROUPS,...  9.85 us
    pallas_call x1, Pallas kernels, per_device(): pl.pallas_call(rest_kernel, out_shape=lines, in_specs=[SMEM, VMEM, VMEM,...  6.51 us
    all_to_all x1, waiting for transfers between devices, per_device(): lax.all_to_all(back, 'slab', split_axis=0, concat_axis=0, tiled=True)  3.56 us
    pallas_call x1, Pallas kernels, per_device(): pl.pallas_call(pack_kernel, out_shape=(jax.ShapeDtypeStruct((PB, 8, TILE)...  3.15 us
    ppermute x1, starting transfers between devices, per_device(): from_below = lax.ppermute(upward, ('slab', 'grp'), down)  2.48 us
  transfers between devices with their start and end apart: 4, of which 1 were waited for; matrix products, arithmetic and copies ran while one was open for 0% of the time, Pallas kernels for 46%

profile of v4, /device:TPU:1, one launch (start us, length us, event | category | flops | bytes accessed | tf_op | source)
XLA Modules:
  0.0 69.0 jit_solution(5096158667864563117)
XLA Ops:
  0.6 3.1 %pack.1 = (f32[64,8,128]{2,1,0:T(8,128)}, f32[64,3,4,128]{3,2,1,0:T(4,128)}) custom-call(s32[1,64]{1,0:T(1,128)} %counts.3, s32[1,64]{1,0:T(1,128)} %owners.3, f32[3,64,128]{2,1,0:T(8,128)} %bitcast.10, f32[64,128]{1,0:T(8,128)} %bitcast.11, f32[64,128]{1,0:T(8,128)} %bitcast.12), custom_call_target="tpu_custom_call" | custom-call | tf_op jit(solution)/shard_map/pack/pallas_call | solution.py:445
  3.8 2.0 %collective-permute-start = (f32[64,8,128]{2,1,0:T(8,128)}, f32[64,8,128]{2,1,0:T(8,128)S(1)}, u32[]{:S(2)}, u32[]{:S(2)}) collective-permute-start(f32[64,8,128]{2,1,0:T(8,128)} %get-tuple-element.14.own), channel_id=1, source_target_pairs={{0,1},{1,2},{2,3},{3,4},{4,5},{5,6},{6,7},{7,8},{8,9},{9,10},{10,1... | collective-permute-start | bytes 786440 | tf_op jit(solution)/shard_map/ppermute | solution.py:465
  5.8 0.0 copy-start.2
  5.8 12.7 %all-to-all-start = ((f32[64,3,4,128]{3,2,1,0:T(4,128)}), f32[64,3,4,128]{3,2,1,0:T(4,128)S(1)}, u32[]{:S(2)}, u32[]{:S(2)}) async-start(f32[64,3,4,128]{3,2,1,0:T(4,128)} %get-tuple-element.19), calls=%async_computation | async-start | bytes 786432 | tf_op jit(solution)/shard_map/all_to_all | solution.py:466
  18.6 0.0 copy-start.3
  18.6 0.0 collective-permute-done.above
  18.6 0.0 copy-done.2
  18.6 0.7 copy-done.3
  19.3 15.1 %cross.1 = (f32[64,128]{1,0:T(8,128)S(1)}, f32[64,128]{1,0:T(8,128)S(1)}, bf16[64,32,128]{2,1,0:T(8,128)(2,1)S(1)}, bf16[64,32,256]{2,1,0:T(8,128)(2,1)S(1)}) custom-call(s32[1,8,64]{2,1,0:T(8,128)S(1)} %bitcast.8, f32[64,8,128]{2,1,0:T(8,128)S(1)} %copy-done.2, f32[64,8,128]{2,1,0:T(8,128)S(1)} %collective-permute-done.above), custom_call_target="tpu_custom_call" | custom-call | flops 10000000000 | bytes 1000000 | tf_op jit(solution)/shard_map/cross/pallas_call | solution.py:469
  34.4 2.5 %collective-permute-start.1 = (f32[64,128]{1,0:T(8,128)S(1)}, f32[64,128]{1,0:T(8,128)S(1)}, u32[]{:S(2)}, u32[]{:S(2)}) collective-permute-start(f32[64,128]{1,0:T(8,128)S(1)} %get-tuple-element.18), channel_id=1, source_target_pairs={{1,0},{2,1},{3,2},{4,3},{5,4},{6,5},{7,6},{8,7},{9,8},{10,9},{11,1... | collective-permute-start | bytes 98312 | tf_op jit(solution)/shard_map/ppermute | solution.py:495
  36.9 0.0 all-to-all-done.got
  36.9 9.9 %potential.1 = (f32[64,2,128]{2,1,0:T(2,128)}, f32[8,128]{1,0:T(8,128)S(1)}, f32[8,128]{1,0:T(8,128)S(1)}) custom-call(s32[1]{0:T(128)} %bitcast.4.place, f32[64,3,4,128]{3,2,1,0:T(4,128)S(1)} %all-to-all-done.got, f32[64,128]{1,0:T(8,128)S(1)} %get-tuple-element.17.after.part), custom_call_target="tpu_custom_call" | custom-call | flops 10000000000 | bytes 1000000 | tf_op jit(solution)/shard_map/potential/pallas_call | solution.py:496
  46.7 10.0 %all-to-all-start.1 = ((f32[64,2,128]{2,1,0:T(2,128)}), f32[64,2,128]{2,1,0:T(2,128)S(1)}, u32[]{:S(2)}, u32[]{:S(2)}) async-start(f32[64,2,128]{2,1,0:T(2,128)} %get-tuple-element.21), calls=%async_computation.1 | async-start | bytes 131072 | tf_op jit(solution)/shard_map/all_to_all | solution.py:530
  56.8 0.0 collective-permute-done.1.below
  56.8 6.5 %rest.1 = f32[64,128]{1,0:T(8,128)} custom-call(s32[1,8,64]{2,1,0:T(8,128)S(1)} %bitcast.9, bf16[64,32,128]{2,1,0:T(8,128)(2,1)S(1)} %get-tuple-element.15.sources, bf16[64,32,256]{2,1,0:T(8,128)(2,1)S(1)} %get-tuple-element.16.targets, f32[64,128]{1,0:T(8,128)S(1)} %get-tuple-element.17.after.part, f32[64,128]{1,0:T(8,128)S(1)} %collective-permute-done.1.below, ...), custom_call_target="tpu_custom_call" | custom-call | flops 10000000000 | bytes 1000000 | tf_op jit(solution)/shard_map/rest/pallas_call | solution.py:520
  63.3 0.0 copy-start
  63.3 0.0 copy-start.1
  63.3 3.6 %all-to-all-done.1.back = f32[64,2,128]{2,1,0:T(2,128)S(1)} async-done(((f32[64,2,128]{2,1,0:T(2,128)}), f32[64,2,128]{2,1,0:T(2,128)S(1)}, u32[]{:S(2)}, u32[]{:S(2)}) %all-to-all-start.1) | async-done | bytes 65568 | tf_op jit(solution)/shard_map/all_to_all | solution.py:530
  66.8 0.0 copy-done
  66.8 0.0 copy-done.1
  66.8 2.1 %unpack.1 = (f32[64,128]{1,0:T(8,128)}, f32[1,128]{1,0:T(1,128)}) custom-call(s32[1]{0:T(128)} %bitcast.4.place, s32[1,64]{1,0:T(1,128)S(1)} %copy-done, s32[1,64]{1,0:T(1,128)S(1)} %copy-done.1, f32[64,2,128]{2,1,0:T(2,128)S(1)} %all-to-all-done.1.back, f32[8,128]{1,0:T(8,128)S(1)} %get-tuple-element.20.after.hot_phi, f32[8,128]{1,0:T(8,128)S(1)} %get-tuple-element.22.energy_in), custom_call_target="tpu_custom_call" | custom-call | tf_op jit(solution)/shard_map/unpack/pallas_call | solution.py:531
Async XLA Ops:
  3.8 14.8 %collective-permute-start = (f32[64,8,128]{2,1,0:T(8,128)}, f32[64,8,128]{2,1,0:T(8,128)S(1)}, u32[]{:S(2)}, u32[]{:S(2)}) collective-permute-start(f32[64,8,128]{2,1,0:T(8,128)} %get-tuple-element.14.own), channel_id=1, source_target_pairs={{0,1},{1,2},{2,3},{3,4},{4,5},{5,6},{6,7},{7,8},{8,9},{9,10},{10,1... | collective-permute-start | bytes 786440 | tf_op jit(solution)/shard_map/ppermute | solution.py:465
  5.8 12.8 %copy-start.2 = (f32[64,8,128]{2,1,0:T(8,128)S(1)}, f32[64,8,128]{2,1,0:T(8,128)}, u32[]{:S(2)}) copy-start(f32[64,8,128]{2,1,0:T(8,128)} %get-tuple-element.14.own) | copy-start | bytes 786436
  5.8 31.1 %all-to-all-start = ((f32[64,3,4,128]{3,2,1,0:T(4,128)}), f32[64,3,4,128]{3,2,1,0:T(4,128)S(1)}, u32[]{:S(2)}, u32[]{:S(2)}) async-start(f32[64,3,4,128]{3,2,1,0:T(4,128)} %get-tuple-element.19), calls=%async_computation | async-start | bytes 786432 | tf_op jit(solution)/shard_map/all_to_all | solution.py:466
  18.6 0.7 %copy-start.3 = (s32[1,64,8]{1,2,0:T(8,128)S(1)}, s32[1,64,8]{1,2,0:T(8,128)}, u32[]{:S(2)}) copy-start(s32[1,64,8]{1,2,0:T(8,128)} %param.9) | copy-start | bytes 6148
  34.4 22.4 %collective-permute-start.1 = (f32[64,128]{1,0:T(8,128)S(1)}, f32[64,128]{1,0:T(8,128)S(1)}, u32[]{:S(2)}, u32[]{:S(2)}) collective-permute-start(f32[64,128]{1,0:T(8,128)S(1)} %get-tuple-element.18), channel_id=1, source_target_pairs={{1,0},{2,1},{3,2},{4,3},{5,4},{6,5},{7,6},{8,7},{9,8},{10,9},{11,1... | collective-permute-start | bytes 98312 | tf_op jit(solution)/shard_map/ppermute | solution.py:495
  46.7 20.1 %all-to-all-start.1 = ((f32[64,2,128]{2,1,0:T(2,128)}), f32[64,2,128]{2,1,0:T(2,128)S(1)}, u32[]{:S(2)}, u32[]{:S(2)}) async-start(f32[64,2,128]{2,1,0:T(2,128)} %get-tuple-element.21), calls=%async_computation.1 | async-start | bytes 131072 | tf_op jit(solution)/shard_map/all_to_all | solution.py:530
  63.3 3.6 %copy-start = (s32[1,64]{1,0:T(1,128)S(1)}, s32[1,64]{1,0:T(1,128)}, u32[]{:S(2)}) copy-start(s32[1,64]{1,0:T(1,128)} %counts.3) | copy-start | bytes 772
  63.3 3.6 %copy-start.1 = (s32[1,64]{1,0:T(1,128)S(1)}, s32[1,64]{1,0:T(1,128)}, u32[]{:S(2)}) copy-start(s32[1,64]{1,0:T(1,128)} %owners.3) | copy-start | bytes 772
